TPU v7x, 32 devices: a whole 2x2x4 slice. The times are simulated.
32 devices in a mesh: dp: 16 (over z, y, x), seq: 2 (over core).
Axes of the slice: x: 2, y: 2, z: 4, core: 2. Of those that a mesh axis runs over, the one named last changes fastest.
Arguments:
- layer_input: bfloat16 [48, 512, 768], P('dp', 'seq'), may hold values from -6 to 6
- gain_attn: bfloat16 [768], P(('dp', 'seq')), may hold values from 0.5 to 1.5
- w_query: bfloat16 [768, 768], P(('dp', 'seq')), may hold values from -0.109375 to 0.109375
- w_key: bfloat16 [768, 768], P(('dp', 'seq')), may hold values from -0.109375 to 0.109375
- w_value: bfloat16 [768, 768], P(('dp', 'seq')), may hold values from -0.21875 to 0.21875
- w_output: bfloat16 [768, 768], P(('dp', 'seq')), may hold values from -0.875 to 0.875
- bias_table: bfloat16 [384], P('dp'), may hold values from -6 to 6
- gain_ffn: bfloat16 [768], P(('dp', 'seq')), may hold values from 0.5 to 1.5
- ffn_in: bfloat16 [768, 3072], P(('dp', 'seq')), may hold values from -0.21875 to 0.21875
- ffn_out: bfloat16 [3072, 768], P(('dp', 'seq')), may hold values from -0.109375 to 0.109375
- buckets: int32 [1023], replicated, may hold values from 0 to 31
- keep_mask: int32 [48, 512], P('dp', 'seq'), may hold values from 0 to 1, as said below
- out_grad: bfloat16 [48, 512, 768], P('dp', 'seq'), may hold values from -6 to 6
Outputs:
- layer_out: bfloat16 [48, 512, 768], P('dp', 'seq')
- grad_input: bfloat16 [48, 512, 768], P('dp', 'seq')
- grad_gain_attn: float32 [768], P(('dp', 'seq'))
- grad_query: float32 [768, 768], P(('dp', 'seq'))
- grad_key: float32 [768, 768], P(('dp', 'seq'))
- grad_value: float32 [768, 768], P(('dp', 'seq'))
- grad_output: float32 [768, 768], P(('dp', 'seq'))
- grad_bias: float32 [384], P('dp')
- grad_gain_ffn: float32 [768], P(('dp', 'seq'))
- grad_ffn_in: float32 [768, 3072], P(('dp', 'seq'))
- grad_ffn_out: float32 [3072, 768], P(('dp', 'seq'))
Inputs may be any that keep to these rules, and one draw needn't show every extreme that they name: `keep_mask`: each sequence's mask is ones up to its length and zeros after it; every length is 64 or more, and among the 3 sequences of each index of dp at least one has no padding.
All inputs are finite; a program needn't handle non-finite values.
Results may differ from a plain program's by a relative error of at most 0.014.
Values may be sent and summed in bfloat16 or wider, within the bound.
No kernel may reach another device: no remote copies, remote signals or barrier semaphores. Data moves between devices by JAX's collectives and lax.ppermute only.
A program may use at most 192 MiB of HBM per device.

v0:
```python
import math

import jax
import jax.numpy as jnp
from jax import lax
from jax.sharding import PartitionSpec as P

HEADS = 12
HEAD_DIM = 64
BUCKETS = 32


EPSILON = 1e-06


def norm_scale(rows):
    return lax.rsqrt(jnp.mean(rows * rows, axis=-1, keepdims=True) + EPSILON)


def norm_back(rows, scale, gain, grad_normed):
    scaled = grad_normed * gain
    inner_mean = jnp.mean(scaled * rows, axis=-1, keepdims=True)
    grad_rows = scale * scaled - rows * (scale * scale * scale) * inner_mean
    grad_gain = jnp.sum(grad_normed * rows * scale, axis=0)
    return (grad_rows, grad_gain)


def bucket_table(buckets, bucket_count):
    padded = jnp.concatenate([buckets, jnp.full((1,), -1, jnp.int32)])
    return (padded[:, None] == jnp.arange(bucket_count, dtype=jnp.int32)[None, :]).astype(
        jnp.float32
    )


def spread_offsets(per_offset, offset_start, rows, cols):
    head_count = per_offset.shape[0]
    window = lax.dynamic_slice_in_dim(per_offset, offset_start, cols + rows, 1)
    repeated = jnp.broadcast_to(window[:, None, :], (head_count, rows, cols + rows))
    repeated = repeated.reshape(head_count, rows * (cols + rows))[:, : rows * (cols + rows - 1)]
    return repeated.reshape(head_count, rows, cols + rows - 1)[:, :, rows - 1 :]


def gather_offsets(grid_grad, offset_start, total_len):
    head_count, rows, cols = grid_grad.shape
    padded = jnp.pad(grid_grad, ((0, 0), (0, 0), (rows - 1, 0)))
    flattened = jnp.pad(padded.reshape(head_count, rows * (cols + rows - 1)), ((0, 0), (0, rows)))
    diagonal_sums = jnp.sum(flattened.reshape(head_count, rows, cols + rows), axis=1)
    empty = jnp.zeros((head_count, total_len), jnp.float32)
    return lax.dynamic_update_slice(empty, diagonal_sums, (jnp.int32(0), offset_start))


def block_scores(query_block, key_block, keep_block, bias_grid):
    product = jnp.einsum(
        "gihd,gjhd->ghij", query_block, key_block, preferred_element_type=jnp.float32
    )
    return product + bias_grid[None] + (keep_block[:, None, None, :] - 1.0) * 1000000000.0


def forward(params, layer_input, keep_mask, buckets):
    gain_attn, w_query, w_key, w_value, w_output, bias_table, gain_ffn, ffn_in, ffn_out = params
    dp_count = lax.axis_size("dp")
    seq_count = lax.axis_size("seq")
    seq_local, local_len, model_width = layer_input.shape
    tok_count = seq_local * local_len
    attn_gain, full_query, full_key, full_value, full_output, table_copies = (
        lax.all_gather(gain_attn, ("dp", "seq"), axis=0, tiled=True),
        lax.all_gather(w_query, ("dp", "seq"), axis=0, tiled=True),
        lax.all_gather(w_key, ("dp", "seq"), axis=0, tiled=True),
        lax.all_gather(w_value, ("dp", "seq"), axis=0, tiled=True),
        lax.all_gather(w_output, ("dp", "seq"), axis=0, tiled=True),
        lax.all_gather(bias_table, ("dp", "seq"), axis=0, tiled=True),
    )
    position_table = (
        table_copies.reshape(dp_count, seq_count, -1)[:, 0]
        .reshape(HEADS, BUCKETS)
        .astype(jnp.float32)
    )
    hidden_in = layer_input.reshape(tok_count, model_width).astype(jnp.float32)
    attn_scale = norm_scale(hidden_in)
    attn_gain = attn_gain.astype(jnp.float32)
    normed_attn = (hidden_in * attn_scale * attn_gain).astype(jnp.bfloat16)

    def project(weight):
        rows = jnp.dot(normed_attn, weight, preferred_element_type=jnp.float32).astype(jnp.bfloat16)
        return rows.reshape(seq_local, local_len, model_width)

    queries = project(full_query)
    key_rows = project(full_key)
    value_rows = project(full_value)
    key_all, value_all, keep_all = (
        lax.all_gather(key_rows, "seq", axis=1, tiled=True),
        lax.all_gather(value_rows, "seq", axis=1, tiled=True),
        lax.all_gather(keep_mask.astype(jnp.bfloat16), "seq", axis=1, tiled=True),
    )
    full_len = key_all.shape[1]
    offset_start = full_len - local_len * (lax.axis_index("seq") + 1)
    one_hot = bucket_table(buckets, BUCKETS)
    per_offset = jnp.einsum("hb,ob->ho", position_table, one_hot, precision=lax.Precision.HIGHEST)
    bias_grid = spread_offsets(per_offset, offset_start, local_len, full_len)
    group_size = math.gcd(seq_local, max(1, 512 // local_len))
    block_count = seq_local // group_size
    query_blocks = queries.reshape(block_count, group_size, local_len, HEADS, HEAD_DIM)
    key_blocks = key_all.reshape(block_count, group_size, full_len, HEADS, HEAD_DIM)
    value_blocks = value_all.reshape(block_count, group_size, full_len, HEADS, HEAD_DIM)
    keep_blocks = keep_all.astype(jnp.float32).reshape(block_count, group_size, full_len)

    def attend(block_args):
        query_block, key_block, value_block, keep_block = block_args
        scores = block_scores(query_block, key_block, keep_block, bias_grid)
        row_max = jnp.max(scores, axis=-1, keepdims=True)
        exp_scores = jnp.exp(scores - row_max)
        row_total = jnp.sum(exp_scores, axis=-1, keepdims=True)
        attn_probs = (exp_scores / row_total).astype(jnp.bfloat16)
        context = jnp.einsum(
            "ghij,gjhd->gihd", attn_probs, value_block, preferred_element_type=jnp.float32
        ).astype(jnp.bfloat16)
        return (context, row_max + jnp.log(row_total))

    context, log_total = lax.map(attend, (query_blocks, key_blocks, value_blocks, keep_blocks))
    context = context.reshape(tok_count, model_width)
    middle = hidden_in + jnp.dot(context, full_output, preferred_element_type=jnp.float32)
    ffn_gain, full_in, full_out = (
        lax.all_gather(gain_ffn, ("dp", "seq"), axis=0, tiled=True),
        lax.all_gather(ffn_in, ("dp", "seq"), axis=0, tiled=True),
        lax.all_gather(ffn_out, ("dp", "seq"), axis=0, tiled=True),
    )
    ffn_gain = ffn_gain.astype(jnp.float32)
    ffn_scale = norm_scale(middle)
    normed_ffn = (middle * ffn_scale * ffn_gain).astype(jnp.bfloat16)
    pre_act = jnp.dot(normed_ffn, full_in, preferred_element_type=jnp.float32)
    activated = jax.nn.gelu(pre_act).astype(jnp.bfloat16)
    layer_out = middle + jnp.dot(activated, full_out, preferred_element_type=jnp.float32)
    return {
        "layer_out": layer_out.astype(jnp.bfloat16).reshape(seq_local, local_len, model_width),
        "attn_gain": attn_gain,
        "full_query": full_query,
        "full_key": full_key,
        "full_value": full_value,
        "full_output": full_output,
        "hidden_in": hidden_in,
        "attn_scale": attn_scale,
        "normed_attn": normed_attn,
        "query_blocks": query_blocks,
        "key_blocks": key_blocks,
        "value_blocks": value_blocks,
        "keep_blocks": keep_blocks,
        "bias_grid": bias_grid,
        "log_total": log_total,
        "context": context,
        "middle": middle,
        "ffn_gain": ffn_gain,
        "full_in": full_in,
        "full_out": full_out,
        "ffn_scale": ffn_scale,
        "normed_ffn": normed_ffn,
        "pre_act": pre_act,
        "activated": activated,
        "one_hot": one_hot,
        "offset_start": offset_start,
    }


def backward(saved, out_grad):
    dp_count = lax.axis_size("dp")
    seq_count = lax.axis_size("seq")
    seq_local, local_len, model_width = out_grad.shape
    tok_count = seq_local * local_len
    grad_rows = out_grad.reshape(tok_count, model_width)
    grad_ffn_out = jnp.einsum(
        "tf,td->fd", saved["activated"], grad_rows, preferred_element_type=jnp.float32
    )
    grad_act = jnp.einsum(
        "td,fd->tf", grad_rows, saved["full_out"], preferred_element_type=jnp.float32
    )
    gelu_pullback = jax.vjp(jax.nn.gelu, saved["pre_act"])[1]
    grad_pre = gelu_pullback(grad_act)[0].astype(jnp.bfloat16)
    grad_ffn_in = jnp.einsum(
        "ti,tf->if", saved["normed_ffn"], grad_pre, preferred_element_type=jnp.float32
    )
    grad_normed_ffn = jnp.einsum(
        "tf,if->ti", grad_pre, saved["full_in"], preferred_element_type=jnp.float32
    )
    grad_middle_norm, grad_gain_ffn = norm_back(
        saved["middle"], saved["ffn_scale"], saved["ffn_gain"], grad_normed_ffn
    )
    grad_middle = grad_rows.astype(jnp.float32) + grad_middle_norm
    ffn_grads = (
        lax.psum_scatter(grad_gain_ffn, ("dp", "seq"), scatter_dimension=0, tiled=True),
        lax.psum_scatter(grad_ffn_in, ("dp", "seq"), scatter_dimension=0, tiled=True),
        lax.psum_scatter(grad_ffn_out, ("dp", "seq"), scatter_dimension=0, tiled=True),
    )
    middle_low = grad_middle.astype(jnp.bfloat16)
    grad_output = jnp.einsum(
        "ti,tj->ij", saved["context"], middle_low, preferred_element_type=jnp.float32
    )
    grad_context = jnp.einsum(
        "tj,ij->ti", middle_low, saved["full_output"], preferred_element_type=jnp.float32
    ).astype(jnp.bfloat16)
    query_blocks = saved["query_blocks"]
    grad_blocks = grad_context.reshape(query_blocks.shape)
    bias_grid = saved["bias_grid"]

    def attend_back(grid_sum, block_args):
        query_block, key_block, value_block, keep_block, log_block, grad_block = block_args
        scores = block_scores(query_block, key_block, keep_block, bias_grid)
        attn_probs = jnp.exp(scores - log_block)
        probs_low = attn_probs.astype(jnp.bfloat16)
        grad_value_rows = jnp.einsum(
            "ghij,gihd->gjhd", probs_low, grad_block, preferred_element_type=jnp.float32
        )
        grad_probs = jnp.einsum(
            "gihd,gjhd->ghij", grad_block, value_block, preferred_element_type=jnp.float32
        )
        grad_scores = attn_probs * (
            grad_probs - jnp.sum(attn_probs * grad_probs, axis=-1, keepdims=True)
        )
        scores_low = grad_scores.astype(jnp.bfloat16)
        grad_query_rows = jnp.einsum(
            "ghij,gjhd->gihd", scores_low, key_block, preferred_element_type=jnp.float32
        ).astype(jnp.bfloat16)
        grad_key_rows = jnp.einsum(
            "ghij,gihd->gjhd", scores_low, query_block, preferred_element_type=jnp.float32
        )
        return (
            grid_sum + jnp.sum(grad_scores, axis=0),
            (grad_query_rows, grad_key_rows, grad_value_rows),
        )

    grid_start = jnp.zeros(bias_grid.shape, jnp.float32)
    grid_grad, (grad_queries, grad_keys, grad_values) = lax.scan(
        attend_back,
        grid_start,
        (
            query_blocks,
            saved["key_blocks"],
            saved["value_blocks"],
            saved["keep_blocks"],
            saved["log_total"],
            grad_blocks,
        ),
    )
    full_len = saved["key_blocks"].shape[2]
    key_sums, value_sums = (
        lax.psum_scatter(
            grad_keys.reshape(seq_local, full_len, model_width).astype(jnp.bfloat16),
            "seq",
            scatter_dimension=1,
            tiled=True,
        ).astype(jnp.float32),
        lax.psum_scatter(
            grad_values.reshape(seq_local, full_len, model_width).astype(jnp.bfloat16),
            "seq",
            scatter_dimension=1,
            tiled=True,
        ).astype(jnp.float32),
    )
    query_low = grad_queries.reshape(tok_count, model_width)
    key_low = key_sums.reshape(tok_count, model_width).astype(jnp.bfloat16)
    value_low = value_sums.reshape(tok_count, model_width).astype(jnp.bfloat16)
    normed_attn = saved["normed_attn"]
    grad_query = jnp.einsum("ti,tj->ij", normed_attn, query_low, preferred_element_type=jnp.float32)
    grad_key = jnp.einsum("ti,tj->ij", normed_attn, key_low, preferred_element_type=jnp.float32)
    grad_value = jnp.einsum("ti,tj->ij", normed_attn, value_low, preferred_element_type=jnp.float32)
    grad_normed_attn = jnp.einsum(
        "tj,ij->ti", query_low, saved["full_query"], preferred_element_type=jnp.float32
    )
    grad_normed_attn = grad_normed_attn + jnp.einsum(
        "tj,ij->ti", key_low, saved["full_key"], preferred_element_type=jnp.float32
    )
    grad_normed_attn = grad_normed_attn + jnp.einsum(
        "tj,ij->ti", value_low, saved["full_value"], preferred_element_type=jnp.float32
    )
    grad_hidden, grad_gain_attn = norm_back(
        saved["hidden_in"], saved["attn_scale"], saved["attn_gain"], grad_normed_attn
    )
    grad_input = (
        (grad_middle + grad_hidden).astype(jnp.bfloat16).reshape(seq_local, local_len, model_width)
    )
    offset_grads = gather_offsets(grid_grad, saved["offset_start"], 2 * full_len)
    bucket_grads = jnp.einsum(
        "ho,ob->hb", offset_grads, saved["one_hot"], precision=lax.Precision.HIGHEST
    ).reshape(-1)
    shard_len = bucket_grads.shape[0] // dp_count
    bias_terms = jnp.broadcast_to(
        bucket_grads.reshape(dp_count, 1, shard_len), (dp_count, seq_count, shard_len)
    ).reshape(-1)
    attn_grads = (
        lax.psum_scatter(grad_gain_attn, ("dp", "seq"), scatter_dimension=0, tiled=True),
        lax.psum_scatter(grad_query, ("dp", "seq"), scatter_dimension=0, tiled=True),
        lax.psum_scatter(grad_key, ("dp", "seq"), scatter_dimension=0, tiled=True),
        lax.psum_scatter(grad_value, ("dp", "seq"), scatter_dimension=0, tiled=True),
        lax.psum_scatter(grad_output, ("dp", "seq"), scatter_dimension=0, tiled=True),
        lax.psum_scatter(bias_terms, ("dp", "seq"), scatter_dimension=0, tiled=True),
    )
    return (grad_input, attn_grads, ffn_grads)


def body(
    layer_input,
    gain_attn,
    w_query,
    w_key,
    w_value,
    w_output,
    bias_table,
    gain_ffn,
    ffn_in,
    ffn_out,
    buckets,
    keep_mask,
    out_grad,
):
    params = (gain_attn, w_query, w_key, w_value, w_output, bias_table, gain_ffn, ffn_in, ffn_out)
    first_pass = forward(params, layer_input, keep_mask, buckets)
    layer_out = first_pass["layer_out"]
    renewed = lax.optimization_barrier((layer_out, params, layer_input, keep_mask))
    saved = forward(renewed[1], renewed[2], renewed[3], buckets)
    grad_input, attn_grads, ffn_grads = backward(saved, out_grad)
    return (
        layer_out,
        grad_input,
        attn_grads[0],
        attn_grads[1],
        attn_grads[2],
        attn_grads[3],
        attn_grads[4],
        attn_grads[5],
        ffn_grads[0],
        ffn_grads[1],
        ffn_grads[2],
    )


def solution(mesh):
    return jax.shard_map(
        body,
        mesh=mesh,
        in_specs=(
            P("dp", "seq", None),
            P(("dp", "seq")),
            P(("dp", "seq"), None),
            P(("dp", "seq"), None),
            P(("dp", "seq"), None),
            P(("dp", "seq"), None),
            P("dp"),
            P(("dp", "seq")),
            P(("dp", "seq"), None),
            P(("dp", "seq"), None),
            P(),
            P("dp", "seq"),
            P("dp", "seq", None),
        ),
        out_specs=(
            P("dp", "seq", None),
            P("dp", "seq", None),
            P(("dp", "seq")),
            P(("dp", "seq"), None),
            P(("dp", "seq"), None),
            P(("dp", "seq"), None),
            P(("dp", "seq"), None),
            P("dp"),
            P(("dp", "seq")),
            P(("dp", "seq"), None),
            P(("dp", "seq"), None),
        ),
        check_vma=False,
    )
```

profile of v0, /device:TPU:0, one launch (start us, length us, event | category | flops | bytes accessed | tf_op | source)
XLA Modules:
  0.0 1613.8 jit_solution(2995659864094457961)
XLA Ops:
  12.0 42.2 %all-reduce.13 = (bf16[768]{0:T(1024)(128)(2,1)S(1)}, bf16[768]{0:T(1024)(128)(2,1)S(1)}, bf16[768]{0:T(1024)(128)(2,1)S(1)}) all-reduce(bf16[768]{0:T(1024)(128)(2,1)S(1)} %dynamic-update-slice, bf16[768]{0:T(1024)(128)(2,1)S(1)} %dynamic-update-slice.1, ...), channel_id=1, replica_groups=mesh['dp'=16,'seq'=2] {'dp','seq'}, use_global_device_ids=true, to_apply=%add.2 | all-reduce | flops 2304 | bytes 9216
  71.2 52.4 %all-gather.23.cloned.1.call-done = bf16[768,768]{1,0:T(8,128)(2,1)} async-done(((bf16[24,768]{1,0:T(8,128)(2,1)}), bf16[768,768]{1,0:T(8,128)(2,1)}) %all-gather.23.cloned.1.call-update) | async-done | bytes 1179664 | tf_op jit(solution)/shard_map/all_gather | solution.py:68
  139.5 16.4 %copy.103 = f32[2,8,256,768]{3,1,2,0:T(8,128)} copy(f32[2,8,256,768]{3,2,1,0:T(8,128)} %bitcast.281) | data formatting | bytes 25165824
  166.2 20.1 %reshape.498 = f32[12,256,767]{2,1,0:T(8,128)} reshape(f32[12,196352]{1,0:T(8,128)} %slice.25) | data formatting | bytes 18849792 | tf_op jit(solution)/shard_map/reshape | solution.py:40
  212.1 61.2 %while.45 = (s32[]{:T(128)}, bf16[3,1,256,12,64]{2,4,3,1,0:T(8,128)(2,1)S(1)}, bf16[3,1,512,12,64]{2,4,3,1,0:T(8,128)(2,1)}, bf16[3,1,256,12,64]{2,4,3,1,0:T(8,1...) while((s32[]{:T(128)}, ...), condition=%wide.region_4.5_spmd, body=%wide.region_1.4_spmd.sunk | while | flops 413864960 | bytes 59019388 | solution.py:119
  280.9 47.5 %all-gather.29.cloned.1.call-done = bf16[768,3072]{1,0:T(8,128)(2,1)} async-done(((bf16[24,3072]{1,0:T(8,128)(2,1)}), bf16[768,3072]{1,0:T(8,128)(2,1)}) %all-gather.29.cloned.1.call-update) | async-done | bytes 4718608 | tf_op jit(solution)/shard_map/all_gather | solution.py:124
  328.5 65.4 %all-gather.31.cloned.1.call-done = bf16[3072,768]{1,0:T(8,128)(2,1)} async-done(((bf16[96,768]{1,0:T(8,128)(2,1)}), bf16[3072,768]{1,0:T(8,128)(2,1)}) %all-gather.31.cloned.1.call-update) | async-done | bytes 4718608 | tf_op jit(solution)/shard_map/all_gather | solution.py:125
  393.9 14.0 add_convert_fusion
  410.0 40.0 %all-reduce.12 = (bf16[768]{0:T(1024)(128)(2,1)S(1)}, bf16[768]{0:T(1024)(128)(2,1)S(1)}, bf16[768]{0:T(1024)(128)(2,1)S(1)}) all-reduce(bf16[768]{0:T(1024)(128)(2,1)S(1)} %dynamic-update-slice.3, bf16[768]{0:T(1024)(128)(2,1)S(1)} %dynamic-update-slice.4, ...), channel_id=1, replica_groups=mesh['dp'=16,'seq'=2] {'dp','seq'}, use_global_device_ids=true, to_apply=%add.5 | all-reduce | flops 2304 | bytes 9216
  464.5 52.3 %all-gather.33.cloned.1.call-done = bf16[768,768]{1,0:T(8,128)(2,1)} async-done(((bf16[24,768]{1,0:T(8,128)(2,1)}), bf16[768,768]{1,0:T(8,128)(2,1)}) %all-gather.33.cloned.1.call-update) | async-done | bytes 1179664 | tf_op jit(solution)/shard_map/all_gather | solution.py:69
  530.8 16.4 %copy.105 = f32[2,8,256,768]{3,1,2,0:T(8,128)} copy(f32[2,8,256,768]{3,2,1,0:T(8,128)} %bitcast.282) | data formatting | bytes 25165824
  557.8 20.3 %reshape.510 = f32[12,256,767]{2,1,0:T(8,128)} reshape(f32[12,196352]{1,0:T(8,128)} %slice.28) | data formatting | bytes 18849792 | tf_op jit(solution)/shard_map/reshape | solution.py:40
  605.3 29.9 %while.46 = (s32[]{:T(128)}, bf16[3,1,256,12,64]{2,4,3,1,0:T(8,128)(2,1)}, f32[3,1,12,256,1]{3,2,4,1,0:T(8,128)}, bf16[3,1,512,12,64]{2,4,3,1,0:T(8,128)(2,1)}, ...) while((s32[]{:T(128)}, ...), condition=%wide.region_10.11_spmd, body=%wide.region_7.10_spmd.sunk | while | flops 415430656 | bytes 27635820 | solution.py:119
  638.7 17.5 %all-gather.43.cloned.1.call-done = bf16[768,768]{1,0:T(8,128)(2,1)} async-done(((bf16[24,768]{1,0:T(8,128)(2,1)}), bf16[768,768]{1,0:T(8,128)(2,1)}) %all-gather.43.cloned.1.call-update) | async-done | bytes 1179664 | tf_op jit(solution)/shard_map/all_gather | solution.py:70
  661.1 60.5 %all-gather.47.cloned.1.call-done = bf16[768,3072]{1,0:T(8,128)(2,1)} async-done(((bf16[24,3072]{1,0:T(8,128)(2,1)}), bf16[768,3072]{1,0:T(8,128)(2,1)}) %all-gather.47.cloned.1.call-update) | async-done | bytes 4718608 | tf_op jit(solution)/shard_map/all_gather | solution.py:124
  732.2 54.7 %all-gather.45.cloned.1.call-done = bf16[3072,768]{1,0:T(8,128)(2,1)} async-done(((bf16[96,768]{1,0:T(8,128)(2,1)}), bf16[3072,768]{1,0:T(8,128)(2,1)}) %all-gather.45.cloned.1.call-update) | async-done | bytes 4718608 | tf_op jit(solution)/shard_map/all_gather | solution.py:125
  818.6 59.1 %while.47 = (s32[]{:T(128)}, f32[12,256,512]{2,1,0:T(8,128)}, bf16[3,1,256,12,64]{2,4,3,1,0:T(8,128)(2,1)}, bf16[3,1,512,12,64]{2,4,3,1,0:T(8,128)(2,1)}, bf16[3...) while((s32[]{:T(128)}, f32[12,256,512]{2,1,0:T(8,128)}, ...), condition=%wide.region_15.16_spmd.clone, body=%wide.region_13.15_spmd.clone.sunk | while | flops 1024129024 | bytes 180608448 | solution.py:230
  941.8 16.6 %reshape.517 = f32[12,196352]{1,0:T(8,128)} reshape(f32[12,256,767]{2,1,0:T(8,128)} %pad.8) | data formatting | bytes 18849792 | tf_op jit(solution)/shard_map/reshape | solution.py:46
  995.5 40.7 %all-reduce.11 = (f32[768]{0:T(1024)}, f32[768]{0:T(1024)}, f32[768]{0:T(1024)}) all-reduce(f32[768]{0:T(1024)S(1)} %get-tuple-element.532, f32[768]{0:T(1024)} %reshape.519, f32[768]{0:T(1024)} %get-tuple-element.530), channel_id=4, replica_groups=mesh['dp'=16,'seq'=2] {'dp','seq'}, use_global_device_ids=true, to_apply=%region_20.21.clone | all-reduce | flops 2304 | bytes 18432
  1044.1 70.9 %reduce-scatter.13.cloned.1.call-done = f32[24,768]{1,0:T(8,128)} async-done(((f32[768,768]{1,0:T(8,128)}), f32[24,768]{1,0:T(8,128)}) %reduce-scatter.13.cloned.1.call-update) | async-done | bytes 73744 | tf_op jit(solution)/shard_map/reduce_scatter | solution.py:289
  1114.9 103.9 %reduce-scatter.17.cloned.1.call-done = f32[24,768]{1,0:T(8,128)} async-done(((f32[768,768]{1,0:T(8,128)}), f32[24,768]{1,0:T(8,128)}) %reduce-scatter.17.cloned.1.call-update) | async-done | bytes 73744 | tf_op jit(solution)/shard_map/reduce_scatter | solution.py:291
  1218.8 104.8 %reduce-scatter.15.cloned.1.call-done = f32[24,768]{1,0:T(8,128)} async-done(((f32[768,768]{1,0:T(8,128)}), f32[24,768]{1,0:T(8,128)}) %reduce-scatter.15.cloned.1.call-update) | async-done | bytes 73744 | tf_op jit(solution)/shard_map/reduce_scatter | solution.py:290
  1323.6 141.0 %reduce-scatter.23.cloned.1.call-done = f32[96,768]{1,0:T(8,128)} async-done(((f32[3072,768]{1,0:T(8,128)}), f32[96,768]{1,0:T(8,128)}) %reduce-scatter.23.cloned.1.call-update) | async-done | bytes 294928 | tf_op jit(solution)/shard_map/reduce_scatter | solution.py:190
  1464.6 142.1 %reduce-scatter.21.cloned.1.call-done = f32[24,3072]{1,0:T(8,128)} async-done(((f32[768,3072]{1,0:T(8,128)}), f32[24,3072]{1,0:T(8,128)}) %reduce-scatter.21.cloned.1.call-update) | async-done | bytes 294928 | tf_op jit(solution)/shard_map/reduce_scatter | solution.py:189
  (378 shorter events, 458.0 us)
Async XLA Ops:
  7.2 60.5 %all-gather.17.cloned.1.call-start = ((), (), s32[]{:S(2)}) async-start(), calls=%async_computation.8 | async-start | bytes 1216512 | tf_op jit(solution)/shard_map/all_gather | solution.py:69
  7.9 115.7 %all-gather.23.cloned.1.call-start = ((), (), s32[]{:S(2)}) async-start(), calls=%async_computation.11 | async-start | bytes 1216512 | tf_op jit(solution)/shard_map/all_gather | solution.py:68
  8.7 186.1 %all-gather.21.cloned.1.call-start = ((), (), s32[]{:S(2)}) async-start(), calls=%async_computation.10 | async-start | bytes 1216512 | tf_op jit(solution)/shard_map/all_gather | solution.py:67
  9.4 195.4 %all-gather.19.cloned.1.call-start = ((), (), s32[]{:S(2)}) async-start(), calls=%async_computation.9 | async-start | bytes 3538944 | tf_op jit(solution)/shard_map/all_gather | solution.py:92
  71.1 138.0 %all-gather.25.cloned.1.call-start = ((), (), s32[]{:S(2)}) async-start(), calls=%async_computation.12 | async-start | bytes 3538944 | tf_op jit(solution)/shard_map/all_gather | solution.py:91
  127.0 150.0 %all-gather.27.cloned.1.call-start = ((), (), s32[]{:S(2)}) async-start(), calls=%async_computation.13 | async-start | bytes 1216512 | tf_op jit(solution)/shard_map/all_gather | solution.py:70
  127.6 200.9 %all-gather.29.cloned.1.call-start = ((), (), s32[]{:S(2)}) async-start(), calls=%async_computation.14 | async-start | bytes 4866048 | tf_op jit(solution)/shard_map/all_gather | solution.py:124
  128.4 265.5 %all-gather.31.cloned.1.call-start = ((), (), s32[]{:S(2)}) async-start(), calls=%async_computation.15 | async-start | bytes 4866048 | tf_op jit(solution)/shard_map/all_gather | solution.py:125
  129.1 331.8 %all-gather.39.cloned.1.call-start = ((), (), s32[]{:S(2)}) async-start(), calls=%async_computation.19 | async-start | bytes 1216512 | tf_op jit(solution)/shard_map/all_gather | solution.py:68
  407.9 108.8 %all-gather.33.cloned.1.call-start = ((), (), s32[]{:S(2)}) async-start(), calls=%async_computation.16 | async-start | bytes 1216512 | tf_op jit(solution)/shard_map/all_gather | solution.py:69
  408.5 177.9 %all-gather.37.cloned.1.call-start = ((), (), s32[]{:S(2)}) async-start(), calls=%async_computation.18 | async-start | bytes 1216512 | tf_op jit(solution)/shard_map/all_gather | solution.py:67
  409.2 187.8 %all-gather.41.cloned.1.call-start = ((), (), s32[]{:S(2)}) async-start(), calls=%async_computation.20 | async-start | bytes 3538944 | tf_op jit(solution)/shard_map/all_gather | solution.py:91
  464.4 135.4 %all-gather.35.cloned.1.call-start = ((), (), s32[]{:S(2)}) async-start(), calls=%async_computation.17 | async-start | bytes 3538944 | tf_op jit(solution)/shard_map/all_gather | solution.py:92
  520.1 136.1 %all-gather.43.cloned.1.call-start = ((), (), s32[]{:S(2)}) async-start(), calls=%async_computation.21 | async-start | bytes 1216512 | tf_op jit(solution)/shard_map/all_gather | solution.py:70
  520.7 200.9 %all-gather.47.cloned.1.call-start = ((), (), s32[]{:S(2)}) async-start(), calls=%async_computation.23 | async-start | bytes 4866048 | tf_op jit(solution)/shard_map/all_gather | solution.py:124
  521.3 265.6 %all-gather.45.cloned.1.call-start = ((), (), s32[]{:S(2)}) async-start(), calls=%async_computation.22 | async-start | bytes 4866048 | tf_op jit(solution)/shard_map/all_gather | solution.py:125
  521.9 376.6 %reduce-scatter.11.cloned.1.call-start = ((), (), s32[]{:S(2)}) async-start(), calls=%async_computation.25 | async-start | bytes 3538944 | tf_op jit(solution)/shard_map/reduce_scatter | solution.py:250
  882.0 22.2 %reduce-scatter.9.cloned.1.call-start = ((), (), s32[]{:S(2)}) async-start(), calls=%async_computation.24 | async-start | bytes 3538944 | tf_op jit(solution)/shard_map/reduce_scatter | solution.py:244
  886.2 157.9 %reduce-scatter.19.cloned.1.call-start = ((), (), s32[]{:S(2)}) async-start(), calls=%async_computation.29 | async-start | bytes 2433024 | tf_op jit(solution)/shard_map/reduce_scatter | solution.py:292
  892.3 222.6 %reduce-scatter.13.cloned.1.call-start = ((), (), s32[]{:S(2)}) async-start(), calls=%async_computation.26 | async-start | bytes 2433024 | tf_op jit(solution)/shard_map/reduce_scatter | solution.py:289
  898.4 320.4 %reduce-scatter.17.cloned.1.call-start = ((), (), s32[]{:S(2)}) async-start(), calls=%async_computation.28 | async-start | bytes 2433024 | tf_op jit(solution)/shard_map/reduce_scatter | solution.py:291
  902.4 421.2 %reduce-scatter.15.cloned.1.call-start = ((), (), s32[]{:S(2)}) async-start(), calls=%async_computation.27 | async-start | bytes 2433024 | tf_op jit(solution)/shard_map/reduce_scatter | solution.py:290
  908.0 556.5 %reduce-scatter.23.cloned.1.call-start = ((), (), s32[]{:S(2)}) async-start(), calls=%async_computation.31 | async-start | bytes 9732096 | tf_op jit(solution)/shard_map/reduce_scatter | solution.py:190
  921.9 684.8 %reduce-scatter.21.cloned.1.call-start = ((), (), s32[]{:S(2)}) async-start(), calls=%async_computation.30 | async-start | bytes 9732096 | tf_op jit(solution)/shard_map/reduce_scatter | solution.py:189
  (74 other events, 1112.8 us)
Sparse Core Ops, SparseCore 0:
  10.9 56.7 all-gather.16
  70.6 52.9 all-gather.22
  126.5 52.9 all-gather.20
  181.5 9.8 all-gather.18
  192.8 12.1 all-gather.24
  207.7 55.2 all-gather.26
  265.9 62.5 all-gather.28
  331.4 62.4 all-gather.30
  408.0 52.8 all-gather.38
  463.7 52.9 all-gather.32
  519.6 52.9 all-gather.36
  574.0 9.8 all-gather.40
  586.1 12.1 all-gather.34
  601.0 55.1 all-gather.42
  659.0 62.5 all-gather.46
  724.4 62.4 all-gather.44
  882.2 8.7 reduce-scatter.10
  893.1 11.0 reduce-scatter.8
  910.1 100.1 reduce-scatter.18
  1016.8 98.0 reduce-scatter.12
  1120.8 97.9 reduce-scatter.16
  1225.5 98.0 reduce-scatter.14
  1330.1 134.4 reduce-scatter.22
  1471.9 134.7 reduce-scatter.20
where the time goes:
time: 1620 us; the launch traced here: 1610 us
  waiting for transfers between devices  942 us (58%)
  local copies, waits for them, and re-layouts  275 us (17%)
  matrix products  218 us (13%)
  blocking collectives  127 us (8%)
  other arithmetic  35.3 us (2%)
    reduce_scatter x1, waiting for transfers between devices, backward(): lax.psum_scatter(grad_ffn_in, ('dp', 'seq'), scatter_dimension=0, tiled=T...  142 us
    reduce_scatter x1, waiting for transfers between devices, backward(): lax.psum_scatter(grad_ffn_out, ('dp', 'seq'), scatter_dimension=0, tiled=...  141 us
    unnamed x3, blocking collectives  123 us
    all_gather x2, waiting for transfers between devices, forward(): lax.all_gather(ffn_out, ('dp', 'seq'), axis=0, tiled=True)  120 us
    all_gather x2, waiting for transfers between devices, forward(): lax.all_gather(ffn_in, ('dp', 'seq'), axis=0, tiled=True)  108 us
    reduce_scatter x1, waiting for transfers between devices, backward(): lax.psum_scatter(grad_key, ('dp', 'seq'), scatter_dimension=0, tiled=True)  105 us
    reduce_scatter x1, waiting for transfers between devices, backward(): lax.psum_scatter(grad_value, ('dp', 'seq'), scatter_dimension=0, tiled=True)  104 us
    unnamed x106, local copies, waits for them, and re-layouts  82.8 us
  transfers between devices with their start and end apart: 24, of which 15 were waited for; matrix products, arithmetic and copies ran while one was open for 25% of the time, Pallas kernels for 0%

commit v1 on v0

v1 whole, which is shorter than its diff:
```python
import functools
import math

import jax
import jax.numpy as jnp
import numpy as np
from jax import lax
from jax.experimental import pallas as pl
from jax.experimental.pallas import tpu as pltpu
from jax.sharding import PartitionSpec as P

HEADS = 12
HEAD_DIM = 64
BUCKETS = 32
EPSILON = 1e-06
LANES = 128
BF = jnp.bfloat16
F32 = jnp.float32
GELU_A = math.sqrt(2.0 / math.pi)
GELU_B = 0.044715

ANY = pl.BlockSpec(memory_space=pl.ANY)
SMEM = pl.BlockSpec(memory_space=pltpu.SMEM)


def whole(shape):
    zeros = (0,) * len(shape)
    return pl.BlockSpec(shape, lambda *_: zeros)


def params(**extra):
    return pltpu.CompilerParams(vmem_limit_bytes=56 * 1024 * 1024, **extra)


def nn(a, b):
    return lax.dot_general(a, b, (((1,), (0,)), ((), ())), preferred_element_type=F32)


def nt(a, b):
    return lax.dot_general(a, b, (((1,), (1,)), ((), ())), preferred_element_type=F32)


def tn(a, b):
    return lax.dot_general(a, b, (((0,), (0,)), ((), ())), preferred_element_type=F32)


def flip(x, axis, bit, count):
    return lax.ppermute(x, axis, [(i, i ^ bit) for i in range(count)])


def gather_pieces(block, cut, dp):
    have = block[None]
    bit = 4
    while bit < dp:
        have = jnp.concatenate([have, flip(have, "dp", bit, dp)], axis=0)
        bit *= 2
    left, right = have[..., :cut], have[..., cut:]
    left_x = flip(left, "dp", 1, dp)
    right_y = flip(right, "dp", 2, dp)
    left_y = flip(left, "dp", 2, dp)
    right_x = flip(right, "dp", 1, dp)
    left_xy = flip(left_x, "dp", 2, dp)
    right_xy = flip(right_y, "dp", 1, dp)
    return [left, left_x, left_y, left_xy], [right, right_x, right_y, right_xy]


def scatter_pieces(left_send, left_keep, right_send, right_keep, dp):
    def add(a, b):
        return (a.astype(F32) + b.astype(F32)).astype(BF)

    left = add(left_keep, flip(left_send, "dp", 2, dp))
    right = add(right_keep, flip(right_send, "dp", 1, dp))
    left = add(left[0], flip(left[1], "dp", 1, dp))
    right = add(right[0], flip(right[1], "dp", 2, dp))
    have = jnp.concatenate([left, right], axis=-1)
    bit = dp // 2
    while bit >= 4:
        half = have.shape[0] // 2
        have = add(have[:half], flip(have[half:], "dp", bit, dp))
        bit //= 2
    return have[0]


def other_core(x):
    return lax.ppermute(x, "seq", [(0, 1), (1, 0)])


def start_blocks(refs, pos, rows, dst, cols, sems):
    copies = []
    at = 0
    for ref in refs:
        for b in range(ref.shape[0]):
            row = pl.multiple_of(pos[at] * rows, rows)
            src = ref.at[b] if cols is None else ref.at[b, :, pl.ds(*cols)]
            copies.append(pltpu.make_async_copy(src, dst.at[pl.ds(row, rows)], sems.at[at]))
            at += 1
    for copy in copies:
        copy.start()
    return copies


def qkv_kernel(meta, pos, x_own, x_oth, buckets, hsel, bsel, *rest, rows, cut, width, nl, nr):
    left, right = rest[:nl], rest[nl : nl + nr]
    q_ref, k_ref, v_ref, norm_ref, misc, peroff, w, sem_l, sem_r, wl, wr = rest[nl + nr :]
    s = meta[0]
    half = width // 2
    depth = w.shape[0]

    @pl.when(pl.program_id(0) == 0)
    def _():
        copies = start_blocks(left, pos, rows, wl, None, sem_l)
        copies += start_blocks(right, pos, rows, wr, None, sem_r)
        for copy in copies:
            copy.wait()
        w[:, :cut] = wl[...]
        w[:, cut:] = wr[...]
        extra = w[:, 3 * half :].astype(F32)
        misc[...] = extra.T[:8]
        spread = (extra[:, 2:3] * bsel[...]).astype(BF)
        table = nn(hsel[s].astype(BF), spread)
        one_hot = (
            lax.broadcasted_iota(jnp.int32, (LANES, buckets.shape[1]), 0) == buckets[...]
        ).astype(F32)
        peroff[...] = nn(table.astype(BF), one_hot.astype(BF))

    gain = misc[0:1, :]
    count = x_own.shape[1]
    for side, x_ref in ((0, x_own), (1, x_oth)):
        x = x_ref[0].astype(F32)
        scale = lax.rsqrt(jnp.mean(x * x, axis=-1, keepdims=True) + EPSILON)
        normed = (x * scale * gain).astype(BF)
        at = pl.ds(pl.multiple_of((s if side == 0 else 1 - s) * count, count), count)
        norm_ref[0, at, :] = normed
        q_ref[0, at, :] = nn(normed, w[:, :half]).astype(BF)
        k_ref[0, at, :] = nn(normed, w[:, half : 2 * half]).astype(BF)
        v_ref[0, at, :] = nn(normed, w[:, 2 * half : 3 * half]).astype(BF)


def lane_half(shape, which):
    lane = lax.broadcasted_iota(jnp.int32, shape, 1)
    return (lane < HEAD_DIM) if which == 0 else (lane >= HEAD_DIM)


def attend_kernel(meta, q_ref, k_ref, v_ref, mask_ref, peroff, own_ref, oth_ref, e_ref, inv_ref, grid, ctx):
    s = meta[0]
    hp = pl.program_id(0)
    length = q_ref.shape[1]
    step = LANES
    span = grid.shape[-1]

    @pl.when(pl.program_id(1) == 0)
    def _():
        for hh in range(2):
            row = peroff[pl.ds(2 * hp + hh, 1), :]
            wide = jnp.broadcast_to(row, (step, span))
            grid[hh] = pltpu.roll(wide, span - step + 1, 1, stride=1, stride_axis=0)

    q, k, v, mask = q_ref[0], k_ref[0], v_ref[0], mask_ref[0]
    zero = jnp.zeros((), BF)
    one = jnp.ones((), BF)
    first = lane_half((length, LANES), 0)
    sums = []
    for hh in range(2):
        keep = first if hh == 0 else ~first
        q_head = jnp.where(keep, q, zero)
        v_head = jnp.where(keep, v, one)
        parts = []
        for a in range(length // step):
            base = length - step - a * step
            scores = nt(q_head[a * step : (a + 1) * step], k)
            scores = scores + grid[hh, :, base : base + length] + mask
            top = jnp.max(scores, axis=-1, keepdims=True)
            low = jnp.exp(scores - top).astype(BF)
            e_ref[0, 0, hh, a * step : (a + 1) * step, :] = low
            parts.append(nn(low, v_head))
        sums.append(jnp.concatenate(parts, axis=0))
    num = jnp.where(first, sums[0], sums[1])
    den = pltpu.roll(jnp.where(first, sums[1], sums[0]), HEAD_DIM, 1)
    inv = 1.0 / den
    inv_ref[0] = inv
    ctx[...] = (num * inv).astype(BF)
    half = length // 2
    own_ref[0] = ctx[pl.ds(pl.multiple_of(s * half, half), half), :]
    oth_ref[0] = ctx[pl.ds(pl.multiple_of((1 - s) * half, half), half), :]


def middle_kernel(meta, pos, x_ref, own_ref, oth_ref, misc, *rest, rows, nb):
    own_w, oth_w = rest[:nb], rest[nb : 2 * nb]
    mid_ref, norm_ref, w, sem_a, sem_b = rest[2 * nb :]
    s = meta[0]
    half = w.shape[2]

    @pl.when(pl.program_id(0) == 0)
    def _():
        copies = start_blocks(own_w, pos, rows, w.at[s], None, sem_a)
        copies += start_blocks(oth_w, pos, rows, w.at[1 - s], None, sem_b)
        for copy in copies:
            copy.wait()

    x = x_ref[0].astype(F32)
    own, oth = own_ref[0], oth_ref[0]
    at_own = pl.ds(pl.multiple_of(s * half, half), half)
    at_oth = pl.ds(pl.multiple_of((1 - s) * half, half), half)
    parts = []
    for c in range(2):
        part = nn(own, w[c, at_own, :]) + nn(oth, w[c, at_oth, :])
        parts.append(x[:, c * half : (c + 1) * half] + part)
    middle = jnp.concatenate(parts, axis=-1)
    mid_ref[0] = middle
    scale = lax.rsqrt(jnp.mean(middle * middle, axis=-1, keepdims=True) + EPSILON)
    norm_ref[0] = (middle * scale * misc[1:2, :]).astype(BF)


def hidden_kernel(pos, own_ref, oth_ref, *rest, rows, cols, nl, nr):
    left, right = rest[:nl], rest[nl : nl + nr]
    act_ref, slope_ref, w, sem_l, sem_r, wl, wr = rest[nl + nr :]

    @pl.when(pl.program_id(0) == 0)
    def _():
        copies = start_blocks(left, pos, rows, wl, cols, sem_l)
        copies += start_blocks(right, pos, rows, wr, None, sem_r)
        for copy in copies:
            copy.wait()
        w[:, : wl.shape[1]] = wl[...]
        w[:, wl.shape[1] :] = wr[...]

    count = own_ref.shape[1]
    width = w.shape[1]
    step = 512 if width % 512 == 0 else width
    for side, ref in ((0, own_ref), (1, oth_ref)):
        for c in range(0, width, step):
            v = nn(ref[0], w[:, c : c + step])
            square = v * v
            t = jnp.tanh(v * (GELU_A + (GELU_A * GELU_B) * square))
            half_up = 0.5 + 0.5 * t
            slope = half_up + (0.5 * v) * (1.0 - t * t) * (GELU_A + (3.0 * GELU_A * GELU_B) * square)
            act_ref[0, side * count : (side + 1) * count, c : c + step] = (v * half_up).astype(BF)
            slope_ref[0, side * count : (side + 1) * count, c : c + step] = slope.astype(BF)


def wgrad_kernel(meta, *rest, na, nb, rows, cut, dp, cols):
    a_refs, b_refs = rest[:na], rest[na : na + nb]
    ls, lk, rs, rk, total = rest[na + nb :]
    mb = a_refs[0].shape[-1]
    i = pl.program_id(0)
    acc = None
    for a_ref, b_ref in zip(a_refs, b_refs):
        a = a_ref[...].reshape(-1, mb)
        b = b_ref[...].reshape(a.shape[0], -1)
        part = tn(a, b)
        acc = part if acc is None else acc + part
    total[pl.ds(pl.multiple_of(i * mb, mb), mb), :] = acc

    @pl.when(i == pl.num_programs(0) - 1)
    def _():
        store_relative(meta, total, ls, lk, rs, rk, rows, cut, dp)


def store_relative(meta, total, ls, lk, rs, rk, rows, cut, dp):
    d = meta[1]
    for rel in range(dp):
        x, y, high = rel & 1, (rel >> 1) & 1, rel >> 2
        at = pl.ds(pl.multiple_of((d ^ rel) * rows, rows), rows)
        (ls if y else lk)[x, high] = total[at, :cut].astype(BF)
        (rs if x else rk)[y, high] = total[at, cut:].astype(BF)


def ffn_back_kernel(pos, g_own, g_oth, slope_ref, w_in, *rest, rows, nl, nr):
    left, right = rest[:nl], rest[nl : nl + nr]
    pre_ref, own_ref, oth_ref, w, sem_l, sem_r, wl, wr = rest[nl + nr :]

    @pl.when(pl.program_id(0) == 0)
    def _():
        copies = start_blocks(left, pos, rows, wl, None, sem_l)
        copies += start_blocks(right, pos, rows, wr, None, sem_r)
        for copy in copies:
            copy.wait()
        w[:, : wl.shape[1]] = wl[...]
        w[:, wl.shape[1] :] = wr[...]

    count = g_own.shape[1]
    width = w.shape[0]
    step = 512 if width % 512 == 0 else width
    for side, ref in ((0, g_own), (1, g_oth)):
        g = ref[0]
        for c in range(0, width, step):
            grad = nt(g, w[c : c + step, :])
            slope = slope_ref[0, side * count : (side + 1) * count, c : c + step].astype(F32)
            pre_ref[0, side * count : (side + 1) * count, c : c + step] = (grad * slope).astype(BF)
        back = nt(pre_ref[0, side * count : (side + 1) * count, :], w_in[...])
        if side == 0:
            own_ref[0] = back
        else:
            oth_ref[0] = back.astype(BF)


def ffn_out_kernel(act_ref, w, own_ref, oth_ref):
    count = own_ref.shape[1]
    own_ref[0] = nn(act_ref[0, :count, :], w[...])
    oth_ref[0] = nn(act_ref[0, count:, :], w[...]).astype(BF)


def middle_back_kernel(meta, g_ref, mid_ref, own_ref, oth_ref, misc, w, gm_ref, low_ref, cown_ref, coth_ref):
    s = meta[0]
    half = w.shape[2]
    middle = mid_ref[0]
    scale = lax.rsqrt(jnp.mean(middle * middle, axis=-1, keepdims=True) + EPSILON)
    grad = own_ref[0] + oth_ref[0].astype(F32)
    scaled = grad * misc[1:2, :]
    inner = jnp.mean(scaled * middle, axis=-1, keepdims=True)
    grad_middle = g_ref[0].astype(F32) + scale * scaled - middle * (scale * scale * scale) * inner
    gm_ref[0] = grad_middle
    low = grad_middle.astype(BF)
    low_ref[0] = low
    for ref, which in ((cown_ref, s), (coth_ref, 1 - s)):
        at = pl.ds(pl.multiple_of(which * half, half), half)
        out = nt(low[:, :half], w[0, at, :]) + nt(low[:, half:], w[1, at, :])
        ref[0] = out.astype(BF)


def wo_grad_kernel(meta, own_ref, oth_ref, low_ref, keep_ref, send_ref, total, *, rows, dp):
    s, d = meta[0], meta[1]
    half = own_ref.shape[-1]
    low = low_ref[...].reshape(-1, low_ref.shape[-1])
    for ref, which in ((own_ref, s), (oth_ref, 1 - s)):
        at = pl.ds(pl.multiple_of(which * half, half), half)
        grad = tn(ref[...].reshape(low.shape[0], half), low)
        total[0, at, :] = grad[:, :half]
        total[1, at, :] = grad[:, half:]
    for rel in range(dp):
        at = pl.ds(pl.multiple_of((d ^ rel) * rows, rows), rows)
        keep_ref[rel] = total[s, at, :].astype(BF)
        send_ref[rel] = total[1 - s, at, :].astype(BF)


def attend_back_kernel(meta, q_ref, k_ref, v_ref, e_ref, inv_ref, own_ref, oth_ref, dq_ref, dk_ref, dv_ref, off_ref, diag, dctx):
    s = meta[0]
    length = q_ref.shape[1]
    half = length // 2
    step = LANES
    n = pl.program_id(1)
    dctx[pl.ds(pl.multiple_of(s * half, half), half), :] = own_ref[0]
    dctx[pl.ds(pl.multiple_of((1 - s) * half, half), half), :] = oth_ref[0]

    @pl.when(n == 0)
    def _():
        diag[...] = jnp.zeros_like(diag)

    q, k, v, inv = q_ref[0], k_ref[0], v_ref[0], inv_ref[0]
    scaled = (dctx[...].astype(F32) * inv).astype(BF)
    zero = jnp.zeros((), BF)
    first = lane_half((length, LANES), 0)
    dq_parts = [None] * (length // step)
    dk = jnp.zeros((length, LANES), F32)
    dv = jnp.zeros((length, LANES), F32)
    for hh in range(2):
        keep = first if hh == 0 else ~first
        q_head, k_head, c_head = (jnp.where(keep, x, zero) for x in (q, k, scaled))
        lane = hh * HEAD_DIM
        for a in range(length // step):
            at = slice(a * step, (a + 1) * step)
            base = length - step - a * step
            low = e_ref[0, 0, hh, at, :]
            e = low.astype(F32)
            term = e * nt(c_head[at], v)
            delta = jnp.sum(term, axis=-1, keepdims=True) * inv[at, lane : lane + 1]
            grad = term - e * delta
            diag[hh, :, base : base + length] += grad
            grad_low = grad.astype(BF)
            part = nn(grad_low, k_head)
            dq_parts[a] = part if hh == 0 else dq_parts[a] + part
            dk = dk + tn(grad_low, q_head[at])
            dv = dv + tn(low, c_head[at])
    dq_ref[0] = jnp.concatenate(dq_parts, axis=0).astype(BF)
    dk_ref[0] = dk.astype(BF)
    dv_ref[0] = dv.astype(BF)

    @pl.when(n == pl.num_programs(1) - 1)
    def _():
        span = diag.shape[-1]
        for hh in range(2):
            acc = jnp.zeros((8, span), F32)
            for g in range(step // 8):
                rows = diag[hh, 8 * g : 8 * g + 8, :]
                shift = step - 8 - 8 * g
                acc = acc + (pltpu.roll(rows, shift, 1) if shift else rows)
            out = acc[7:8]
            for b in range(7):
                out = out + pltpu.roll(acc[b : b + 1], 7 - b, 1)
            off_ref[0, hh : hh + 1, :] = out


def qkv_grad_kernel(meta, norm_ref, dq_ref, dk_ref, dv_ref, off_ref, buckets, hsel, bsel, ls, lk, rs, rk, total, *, rows, cut, dp):
    s = meta[0]
    i = pl.program_id(0)
    mb = norm_ref.shape[-1]
    half = dq_ref.shape[-1]
    a = norm_ref[...].reshape(-1, mb)
    at = pl.ds(pl.multiple_of(i * mb, mb), mb)
    for c, ref in enumerate((dq_ref, dk_ref, dv_ref)):
        total[at, c * half : (c + 1) * half] = tn(a, ref[...].reshape(a.shape[0], half))

    @pl.when(i == pl.num_programs(0) - 1)
    def _():
        one_hot = (
            lax.broadcasted_iota(jnp.int32, (LANES, buckets.shape[1]), 0) == buckets[...]
        ).astype(F32)
        per_bucket = lax.dot_general(
            off_ref[...], one_hot, (((1,), (1,)), ((), ())), precision=lax.Precision.HIGHEST, preferred_element_type=F32
        )
        spread = lax.dot_general(
            hsel[s], per_bucket, (((0,), (0,)), ((), ())), precision=lax.Precision.HIGHEST, preferred_element_type=F32
        )
        column = jnp.sum(spread * bsel[...], axis=-1, keepdims=True)
        total[:, 3 * half :] = jnp.broadcast_to(column, (column.shape[0], LANES))
        store_relative(meta, total, ls, lk, rs, rk, rows, cut, dp)


def input_grad_kernel(meta, dq_ref, dk_ref, dv_ref, w, own_ref, oth_ref):
    s = meta[0]
    half = dq_ref.shape[-1]
    count = own_ref.shape[1]
    for side, ref in ((0, own_ref), (1, oth_ref)):
        at = pl.ds(pl.multiple_of((s if side == 0 else 1 - s) * count, count), count)
        out = nt(dq_ref[0, at, :], w[:, :half])
        out = out + nt(dk_ref[0, at, :], w[:, half : 2 * half])
        out = out + nt(dv_ref[0, at, :], w[:, 2 * half : 3 * half])
        ref[0] = out.astype(ref.dtype)


def last_kernel(x_ref, gm_ref, own_ref, oth_ref, misc, out_ref):
    x = x_ref[0].astype(F32)
    scale = lax.rsqrt(jnp.mean(x * x, axis=-1, keepdims=True) + EPSILON)
    scaled = (own_ref[0] + oth_ref[0].astype(F32)) * misc[0:1, :]
    inner = jnp.mean(scaled * x, axis=-1, keepdims=True)
    out_ref[0] = (gm_ref[0] + scale * scaled - x * (scale * scale * scale) * inner).astype(BF)


def body(
    layer_input,
    gain_attn,
    w_query,
    w_key,
    w_value,
    w_output,
    bias_table,
    gain_ffn,
    ffn_in,
    ffn_out,
    buckets,
    keep_mask,
    out_grad,
):
    dp = lax.axis_size("dp")
    s = lax.axis_index("seq")
    d = lax.axis_index("dp")
    nseq, count, width = layer_input.shape
    length = 2 * count
    span = 2 * length
    half = width // 2
    shard = w_query.shape[0]
    rows = 2 * shard
    hid_rows = ffn_out.shape[0]
    hid = hid_rows * dp
    table_rows = bias_table.shape[0]
    tok = nseq * length
    pairs = half // LANES
    meta = jnp.stack([s, d]).astype(jnp.int32)
    aligned = rows % 16 == 0 and hid_rows % 16 == 0

    def sds(shape, dtype=BF):
        return jax.ShapeDtypeStruct(shape, dtype)

    def columns(h):
        cut = [lax.dynamic_slice_in_dim(w, h * half, half, 1) for w in (w_query, w_key, w_value)]
        table = jnp.pad(bias_table, (0, shard - table_rows))
        extra = jnp.stack([gain_attn, gain_ffn, table], axis=1)
        extra = jnp.pad(extra, ((0, 0), (0, LANES - 3)))
        out_cols = lax.dynamic_slice_in_dim(w_output, h * half, half, 1)
        in_cols = lax.dynamic_index_in_dim(ffn_in.reshape(shard, dp, 2, hid_rows), h, 2, keepdims=False)
        return jnp.concatenate(cut + [extra, out_cols, in_cols.reshape(shard, hid)], axis=1)

    mine, theirs = columns(s), other_core(columns(1 - s))
    joined = jnp.where(s == 0, jnp.concatenate([mine, theirs]), jnp.concatenate([theirs, mine]))
    x_oth = other_core(layer_input)
    g_oth = other_core(out_grad)
    keep_oth = other_core(keep_mask.astype(BF))
    keep = keep_mask.astype(BF)
    keep = jnp.where(s == 0, jnp.concatenate([keep, keep_oth], 1), jnp.concatenate([keep_oth, keep], 1))
    mask = ((keep.astype(F32) - 1.0) * 1e9)[:, None, :]
    first_cols = 3 * half + LANES
    first_cut = (first_cols // LANES // 2) * LANES
    second_cut = ((half + hid) // LANES // 2) * LANES
    third_cut = (width // LANES // 2) * LANES

    first_l, first_r = gather_pieces(joined[:, :first_cols], first_cut, dp)
    second_l, second_r = gather_pieces(joined[:, first_cols:], second_cut, dp)
    third_l, third_r = gather_pieces(ffn_out, third_cut, dp)

    high = dp // 4
    relative = np.array([(h << 2) | low for low in range(4) for h in range(high)], np.int32)
    pos = (d ^ jnp.asarray(relative)).astype(jnp.int32)

    def settle(pieces, cols=None):
        if aligned:
            return pieces
        every = jnp.concatenate(pieces, axis=0)
        order = jnp.argsort(pos)
        return [every[order].reshape(1, -1, every.shape[-1])]

    if not aligned:
        pos_k, rows_k, hid_rows_k, nblk, dp_k = jnp.zeros((1,), jnp.int32), width, hid, 1, 1
    else:
        pos_k, rows_k, hid_rows_k, nblk, dp_k = pos, rows, hid_rows, dp, dp

    feature = np.arange(width)
    chunk, within = feature // rows, feature % rows
    entry = np.where(within % shard < table_rows, table_rows * chunk + within % shard, -1)
    head, bucket = entry // BUCKETS, entry % BUCKETS
    half_heads = HEADS // 2
    hsel = np.zeros((2, 8, width), np.float32)
    bsel = np.zeros((width, LANES), np.float32)
    for f in range(width):
        if entry[f] >= 0:
            hsel[head[f] // half_heads, head[f] % half_heads, f] = 1.0
            bsel[f, bucket[f]] = 1.0
    bsel_once = jnp.asarray(np.where(within[:, None] < shard, bsel, 0.0))
    hsel, bsel = jnp.asarray(hsel), jnp.asarray(bsel)
    padded = jnp.concatenate([buckets, jnp.full((span - buckets.shape[0],), -1, jnp.int32)])[None]

    a_l, a_r = settle(first_l), settle(first_r)
    seq_block = lambda shape: pl.BlockSpec((1,) + shape, lambda n: (n, 0, 0))
    q, k, v, normed_attn, misc, peroff, w_qkv = pl.pallas_call(
        functools.partial(
            qkv_kernel, rows=rows_k, cut=first_cut, width=width, nl=len(a_l), nr=len(a_r)
        ),
        grid=(nseq,),
        in_specs=[SMEM, SMEM, seq_block((count, width)), seq_block((count, width)), whole((1, span)), whole(hsel.shape), whole(bsel.shape)]
        + [ANY] * (len(a_l) + len(a_r)),
        out_specs=[seq_block((length, half))] * 3
        + [seq_block((length, width)), whole((8, width)), whole((8, span)), whole((width, first_cols))],
        out_shape=[sds((nseq, length, half))] * 3
        + [sds((nseq, length, width)), sds((8, width), F32), sds((8, span), F32), sds((width, first_cols))],
        scratch_shapes=[
            pltpu.SemaphoreType.DMA((nblk,)),
            pltpu.SemaphoreType.DMA((nblk,)),
            pltpu.VMEM((width, first_cut), BF),
            pltpu.VMEM((width, first_cols - first_cut), BF),
        ],
        compiler_params=params(),
        name="qkv",
    )(meta, pos_k, layer_input, x_oth, padded, hsel, bsel_once, *a_l, *a_r)

    pair = pl.BlockSpec((1, length, LANES), lambda h, n: (n, 0, h))
    pair_half = pl.BlockSpec((1, count, LANES), lambda h, n: (n, 0, h))
    e_block = pl.BlockSpec((1, 1, 2, length, length), lambda h, n: (n, h, 0, 0, 0))
    ctx_own, ctx_send, expo, inv = pl.pallas_call(
        attend_kernel,
        grid=(pairs, nseq),
        in_specs=[SMEM, pair, pair, pair, pl.BlockSpec((1, 1, length), lambda h, n: (n, 0, 0)), whole((8, span))],
        out_specs=[pair_half, pair_half, e_block, pair],
        out_shape=[
            sds((nseq, count, half)),
            sds((nseq, count, half)),
            sds((nseq, pairs, 2, length, length)),
            sds((nseq, length, half), F32),
        ],
        scratch_shapes=[pltpu.VMEM((2, LANES, span), F32), pltpu.VMEM((length, LANES), BF)],
        compiler_params=params(),
        name="attend",
    )(meta, q, k, v, mask, peroff)
    ctx_oth = other_core(ctx_send)

    wo_own = jnp.concatenate([x[..., :half] for x in second_l], axis=0)
    wo_oth = other_core(wo_own)
    wo_own, wo_oth = settle([wo_own]), settle([wo_oth])
    middle, normed_ffn, w_o = pl.pallas_call(
        functools.partial(middle_kernel, rows=rows_k, nb=1),
        grid=(nseq,),
        in_specs=[SMEM, SMEM, seq_block((count, width)), seq_block((count, half)), seq_block((count, half)), whole((8, width)), ANY, ANY],
        out_specs=[seq_block((count, width)), seq_block((count, width)), whole((2, width, half))],
        out_shape=[sds((nseq, count, width), F32), sds((nseq, count, width)), sds((2, width, half))],
        scratch_shapes=[pltpu.SemaphoreType.DMA((nblk,)), pltpu.SemaphoreType.DMA((nblk,))],
        compiler_params=params(),
        name="middle",
    )(meta, pos_k, layer_input, ctx_own, ctx_oth, misc, *wo_own, *wo_oth)
    normed_oth = other_core(normed_ffn)

    b_l, b_r = settle(second_l), settle(second_r)
    act, slope, w_in = pl.pallas_call(
        functools.partial(
            hidden_kernel, rows=rows_k, cols=(half, second_cut - half), nl=len(b_l), nr=len(b_r)
        ),
        grid=(nseq,),
        in_specs=[SMEM, seq_block((count, width)), seq_block((count, width))] + [ANY] * (len(b_l) + len(b_r)),
        out_specs=[seq_block((length, hid)), seq_block((length, hid)), whole((width, hid))],
        out_shape=[sds((nseq, length, hid)), sds((nseq, length, hid)), sds((width, hid))],
        scratch_shapes=[
            pltpu.SemaphoreType.DMA((nblk,)),
            pltpu.SemaphoreType.DMA((nblk,)),
            pltpu.VMEM((width, second_cut - half), BF),
            pltpu.VMEM((width, half + hid - second_cut), BF),
        ],
        compiler_params=params(),
        name="hidden",
    )(pos_k, normed_ffn, normed_oth, *b_l, *b_r)

    def block_outs(block_rows, cut, cols):
        if aligned:
            left, right = (2, high, block_rows, cut), (2, high, block_rows, cols - cut)
            return [left, left, right, right]
        return [(dp * block_rows, cols)]

    def in_relative(parts, block_rows, cut):
        if aligned:
            return parts
        blocks = parts[0].reshape(dp, block_rows, -1)[pos].reshape(2, 2, high, block_rows, -1)
        left, right = blocks[..., :cut], blocks[..., cut:]
        return left[1], left[0], right[:, 1], right[:, 0]

    def whole_wgrad(meta, *rest, na, nb, **_):
        a_refs, b_refs = rest[:na], rest[na : na + nb]
        out = rest[na + nb]
        acc = None
        for a_ref, b_ref in zip(a_refs, b_refs):
            a = a_ref[...].reshape(-1, a_ref.shape[-1])
            part = tn(a, b_ref[...].reshape(a.shape[0], -1))
            acc = part if acc is None else acc + part
        out[...] = acc.astype(BF)

    def wgrad(a_list, b_list, block_rows, cut, name):
        m, cols = a_list[0].shape[-1], b_list[0].shape[-1]
        mb = 384
        shapes = block_outs(block_rows, cut, cols)
        kernel = wgrad_kernel if aligned else whole_wgrad
        out_specs = [whole(x) for x in shapes] if aligned else [pl.BlockSpec((mb, cols), lambda i: (i, 0))]
        return in_relative(
            pl.pallas_call(
                functools.partial(kernel, na=len(a_list), nb=len(b_list), rows=block_rows, cut=cut, dp=dp, cols=cols),
                grid=(m // mb,),
                in_specs=[SMEM]
                + [pl.BlockSpec(a.shape[:2] + (mb,), lambda i: (0, 0, i)) for a in a_list]
                + [whole(b.shape) for b in b_list],
                out_specs=out_specs,
                out_shape=[sds(x) for x in shapes],
                scratch_shapes=[pltpu.VMEM((m, cols), F32)] if aligned else [],
                compiler_params=params(),
                name=name,
            )(meta, *a_list, *b_list),
            block_rows,
            cut,
        )

    act_own, act_oth = act[:, :count], act[:, count:]
    grad_out_parts = wgrad([act_own, act_oth], [out_grad, g_oth], hid_rows, third_cut, "grad_ffn_out")
    grad_ffn_out = scatter_pieces(*grad_out_parts, dp).astype(F32)

    c_l, c_r = settle(third_l), settle(third_r)
    grad_pre, back_own, back_send, w_out = pl.pallas_call(
        functools.partial(ffn_back_kernel, rows=hid_rows_k, nl=len(c_l), nr=len(c_r)),
        grid=(nseq,),
        in_specs=[SMEM, seq_block((count, width)), seq_block((count, width)), seq_block((length, hid)), whole((width, hid))]
        + [ANY] * (len(c_l) + len(c_r)),
        out_specs=[seq_block((length, hid)), seq_block((count, width)), seq_block((count, width)), whole((hid, width))],
        out_shape=[sds((nseq, length, hid)), sds((nseq, count, width), F32), sds((nseq, count, width)), sds((hid, width))],
        scratch_shapes=[
            pltpu.SemaphoreType.DMA((nblk,)),
            pltpu.SemaphoreType.DMA((nblk,)),
            pltpu.VMEM((hid, third_cut), BF),
            pltpu.VMEM((hid, width - third_cut), BF),
        ],
        compiler_params=params(),
        name="ffn_back",
    )(pos_k, out_grad, g_oth, slope, w_in, *c_l, *c_r)
    back_oth = other_core(back_send)

    pre_own, pre_oth = grad_pre[:, :count], grad_pre[:, count:]
    in_cut = (hid // LANES // 2) * LANES
    grad_in_parts = wgrad([normed_ffn, normed_oth], [pre_own, pre_oth], rows, in_cut, "grad_ffn_in")
    grad_in_block = scatter_pieces(*grad_in_parts, dp)

    out_own, out_send = pl.pallas_call(
        ffn_out_kernel,
        grid=(nseq,),
        in_specs=[seq_block((length, hid)), whole((hid, width))],
        out_specs=[seq_block((count, width)), seq_block((count, width))],
        out_shape=[sds((nseq, count, width), F32), sds((nseq, count, width))],
        compiler_params=params(),
        name="ffn_out",
    )(act, w_out)
    layer_out = (middle + out_own + other_core(out_send).astype(F32)).astype(BF)

    grad_middle, middle_low, dctx_own, dctx_send = pl.pallas_call(
        middle_back_kernel,
        grid=(nseq,),
        in_specs=[SMEM] + [seq_block((count, width))] * 4 + [whole((8, width)), whole((2, width, half))],
        out_specs=[seq_block((count, width)), seq_block((count, width)), seq_block((count, half)), seq_block((count, half))],
        out_shape=[
            sds((nseq, count, width), F32),
            sds((nseq, count, width)),
            sds((nseq, count, half)),
            sds((nseq, count, half)),
        ],
        compiler_params=params(),
        name="middle_back",
    )(meta, out_grad, middle, back_own, back_oth, misc, w_o)
    dctx_oth = other_core(dctx_send)

    rel_meta = meta if aligned else jnp.stack([s, jnp.zeros_like(d)]).astype(jnp.int32)
    wo_keep, wo_send = pl.pallas_call(
        functools.partial(wo_grad_kernel, rows=rows_k, dp=dp_k),
        out_shape=[sds((dp_k, rows_k, half))] * 2,
        in_specs=[SMEM, whole(ctx_own.shape), whole(ctx_oth.shape), whole(middle_low.shape)],
        out_specs=[whole((dp_k, rows_k, half))] * 2,
        scratch_shapes=[pltpu.VMEM((2, width, half), F32)],
        grid=(1,),
        compiler_params=params(),
        name="grad_output",
    )(rel_meta, ctx_own, ctx_oth, middle_low)
    wo_sum = (wo_keep.astype(F32) + other_core(wo_send).astype(F32)).astype(BF)
    if not aligned:
        wo_sum = wo_sum.reshape(dp, rows, half)[d ^ jnp.arange(dp)]
    wo_cut = (half // LANES // 2) * LANES
    by_bits = wo_sum.reshape(high, 2, 2, rows, half)
    wo_left = jnp.swapaxes(by_bits[..., :wo_cut], 0, 2)
    wo_right = jnp.moveaxis(by_bits[..., wo_cut:], 0, 2)
    wo_parts = (wo_left[:, 1], wo_left[:, 0], wo_right[:, 1], wo_right[:, 0])
    wo_block = scatter_pieces(*wo_parts, dp)

    dq, dk, dv, off = pl.pallas_call(
        attend_back_kernel,
        grid=(pairs, nseq),
        in_specs=[SMEM, pair, pair, pair, e_block, pair, pair_half, pair_half],
        out_specs=[pair, pair, pair, pl.BlockSpec((1, 2, span), lambda h, n: (h, 0, 0))],
        out_shape=[sds((nseq, length, half))] * 3 + [sds((pairs, 2, span), F32)],
        scratch_shapes=[pltpu.VMEM((2, LANES, span), F32), pltpu.VMEM((length, LANES), BF)],
        compiler_params=params(),
        name="attend_back",
    )(meta, q, k, v, expo, inv, dctx_own, dctx_oth)
    off = jnp.pad(off.reshape(half_heads, span), ((0, 8 - half_heads), (0, 0)))

    mb = 384
    shapes = block_outs(rows, first_cut, first_cols)
    whole_shapes = shapes if aligned else [(width, first_cols)]

    def qkv_whole(meta, *rest):
        ins, out, total = rest[:8], rest[8], rest[9]
        qkv_grad_kernel(meta, *ins, None, None, None, None, total, rows=width, cut=first_cut, dp=0)
        out[...] = total[...].astype(BF)

    qkv_parts = in_relative(
        pl.pallas_call(
            functools.partial(qkv_grad_kernel, rows=rows, cut=first_cut, dp=dp) if aligned else qkv_whole,
            grid=(width // mb,),
            in_specs=[SMEM, pl.BlockSpec((nseq, length, mb), lambda i: (0, 0, i))]
            + [whole((nseq, length, half))] * 3
            + [whole((8, span)), whole((1, span)), whole(hsel.shape), whole(bsel.shape)],
            out_specs=[whole(x) for x in whole_shapes],
            out_shape=[sds(x) for x in whole_shapes],
            scratch_shapes=[pltpu.VMEM((width, first_cols), F32)],
            compiler_params=params(),
            name="grad_qkv",
        )(meta, normed_attn, dq, dk, dv, off, padded, hsel, bsel),
        rows,
        first_cut,
    )
    qkv_block = scatter_pieces(*qkv_parts, dp)

    dn_own, dn_send = pl.pallas_call(
        input_grad_kernel,
        grid=(nseq,),
        in_specs=[SMEM] + [seq_block((length, half))] * 3 + [whole((width, first_cols))],
        out_specs=[seq_block((count, width)), seq_block((count, width))],
        out_shape=[sds((nseq, count, width), F32), sds((nseq, count, width))],
        compiler_params=params(),
        name="input_grad",
    )(meta, dq, dk, dv, w_qkv)
    grad_input = pl.pallas_call(
        last_kernel,
        grid=(nseq,),
        in_specs=[seq_block((count, width))] * 4 + [whole((8, width))],
        out_specs=seq_block((count, width)),
        out_shape=sds((nseq, count, width)),
        compiler_params=params(),
        name="last",
    )(layer_input, grad_middle, dn_own, other_core(dn_send), misc)

    def both_cores(block):
        mine = lax.dynamic_slice_in_dim(block, s * shard, shard, 0)
        theirs = other_core(lax.dynamic_slice_in_dim(block, (1 - s) * shard, shard, 0))
        first, last = jnp.where(s == 0, mine, theirs), jnp.where(s == 0, theirs, mine)
        return first.astype(F32), last.astype(F32)

    in_first, in_last = both_cores(grad_in_block)
    grad_ffn_in = jnp.stack(
        [in_first.reshape(shard, dp, hid_rows), in_last.reshape(shard, dp, hid_rows)], axis=2
    ).reshape(shard, 2 * hid)
    wo_first, wo_last = both_cores(wo_block)
    grad_output = jnp.concatenate([wo_first, wo_last], axis=1)
    qkv_first, qkv_last = both_cores(qkv_block)
    grad_query, grad_key, grad_value = (
        jnp.concatenate([x[:, c * half : (c + 1) * half] for x in (qkv_first, qkv_last)], axis=1)
        for c in range(3)
    )
    grad_gain_attn = sum(
        jnp.sum(w.astype(F32) * g, axis=1)
        for w, g in ((w_query, grad_query), (w_key, grad_key), (w_value, grad_value))
    ) / gain_attn.astype(F32)
    grad_gain_ffn = jnp.sum(ffn_in.astype(F32) * grad_ffn_in, axis=1) / gain_ffn.astype(F32)
    bias_cols = jnp.where(2 * d < dp, qkv_first[:, 3 * half], qkv_last[:, 3 * half])
    grad_bias = bias_cols[:table_rows]
    return (
        layer_out,
        grad_input,
        grad_gain_attn,
        grad_query,
        grad_key,
        grad_value,
        grad_output,
        grad_bias,
        grad_gain_ffn,
        grad_ffn_in,
        grad_ffn_out,
    )


def solution(mesh):
    both = ("dp", "seq")
    return jax.shard_map(
        body,
        mesh=mesh,
        in_specs=(
            P("dp", "seq", None),
            P(both),
            P(both, None),
            P(both, None),
            P(both, None),
            P(both, None),
            P("dp"),
            P(both),
            P(both, None),
            P(both, None),
            P(),
            P("dp", "seq"),
            P("dp", "seq", None),
        ),
        out_specs=(
            P("dp", "seq", None),
            P("dp", "seq", None),
            P(both),
            P(both, None),
            P(both, None),
            P(both, None),
            P(both, None),
            P("dp"),
            P(both),
            P(both, None),
            P(both, None),
        ),
        check_vma=False,
    )
```

time: 1620 us -> 411 us (0.25)
  waiting for transfers between devices: 942 us -> 147 us
  local copies, waits for them, and re-layouts: 275 us -> 24.2 us
  matrix products: 218 us -> 0 us
  Pallas kernels: 0 us -> 161 us
  blocking collectives: 127 us -> 0 us
  starting transfers between devices: 1.13 us -> 57.8 us
  other arithmetic: 35.3 us -> 17.7 us
    reduce_scatter x8 -> x0, waiting for transfers between devices: 564 us -> none  [the longest x1 142 us: backward(): lax.psum_scatter(grad_ffn_in, ('dp', 'seq'), scatter_dimension=0, tiled=T...]
    all_gather x16 -> x0, waiting for transfers between devices: 371 us -> none  [the longest x2 120 us: forward(): lax.all_gather(ffn_out, ('dp', 'seq'), axis=0, tiled=True)]
    dot_general x52 -> x0, matrix products: 218 us -> none  [the longest x6 42.5 us: attend(): jnp.einsum('ghij,gjhd->gihd', attn_probs, value_block, preferred_element_...]
    pallas_call x0 -> x14, Pallas kernels: none -> 161 us  [the longest x1 34.6 us: body(): pl.pallas_call(attend_back_kernel, grid=(pairs, nseq), in_specs=[SMEM, pa...]
    ppermute x0 -> x63, waiting for transfers between devices: none -> 147 us  [the longest x48 145 us: flip(): return lax.ppermute(x, axis, [(i, i ^ bit) for i in range(count)])]
    unnamed x3 -> x0, blocking collectives: 123 us -> none
    unnamed x106 -> x117, local copies, waits for them, and re-layouts: 82.8 us -> 7.31 us
    reshape x9 -> x6, local copies, waits for them, and re-layouts: 63.1 us -> 2.99 us  [the longest x1 1.12 us: columns(): ffn_in.reshape(shard, dp, 2, hid_rows)]
  transfers between devices with their start and end apart: 24 -> 63, of which waited for: 15 -> 31; matrix products, arithmetic and copies ran while one was open for 25% -> 8% of each run, Pallas kernels for 0% -> 31%
where the time goes in v1:
time: 411 us; the launch traced here: 410 us
  Pallas kernels  161 us (39%)
  waiting for transfers between devices  147 us (36%)
  starting transfers between devices  57.8 us (14%)
  local copies, waits for them, and re-layouts  24.2 us (6%)
  other arithmetic  17.7 us (4%)
    ppermute x48, waiting for transfers between devices, flip(): return lax.ppermute(x, axis, [(i, i ^ bit) for i in range(count)])  145 us
    ppermute x48, starting transfers between devices, flip(): return lax.ppermute(x, axis, [(i, i ^ bit) for i in range(count)])  55.4 us
    pallas_call x1, Pallas kernels, body(): pl.pallas_call(attend_back_kernel, grid=(pairs, nseq), in_specs=[SMEM, pa...  34.6 us
    pallas_call x1, Pallas kernels, body(): pl.pallas_call(attend_kernel, grid=(pairs, nseq), in_specs=[SMEM, pair, p...  24.7 us
    pallas_call x2, Pallas kernels, wgrad(): pl.pallas_call(functools.partial(kernel, na=len(a_list), nb=len(b_list),...  17.1 us
    pallas_call x1, Pallas kernels, body(): pl.pallas_call(functools.partial(ffn_back_kernel, rows=hid_rows_k, nl=len...  14.7 us
    pallas_call x1, Pallas kernels, body(): pl.pallas_call(functools.partial(hidden_kernel, rows=rows_k, cols=(half,...  12.6 us
    pallas_call x1, Pallas kernels, body(): pl.pallas_call(functools.partial(qkv_kernel, rows=rows_k, cut=first_cut,...  10 us
  transfers between devices with their start and end apart: 63, of which 31 were waited for; matrix products, arithmetic and copies ran while one was open for 8% of the time, Pallas kernels for 31%

profile of v1, /device:TPU:0, one launch (start us, length us, event | category | flops | bytes accessed | tf_op | source)
XLA Modules:
  0.0 410.0 jit_solution(3979348481280973125)
XLA Ops:
  20.1 16.1 %collective-permute-done.3 = bf16[2,48,1280]{2,1,0:T(8,128)(2,1)S(1)} collective-permute-done((bf16[2,48,1280]{2,1,0:T(8,128)(2,1)S(1)}, bf16[2,48,1280]{2,1,0:T(8,128)(2,1)S(1)}, u32[]{:S(2)}, u32[]{:S(2)}) %collective-permute-start.3) | collective-permute-done | bytes 245792 | tf_op jit(solution)/shard_map/ppermute | solution.py:48
  47.2 6.1 %collective-permute-done.14.rest_1_ = bf16[4,48,896]{2,1,0:T(8,128)(2,1)} collective-permute-done((bf16[4,48,896]{2,1,0:T(8,128)(2,1)S(1)}, bf16[4,48,896]{2,1,0:T(8,128)(2,1)}, u32[]{:S(2)}, u32[]{:S(2)}) %collective-permute-start.14) | collective-permute-done | bytes 344096 | tf_op jit(solution)/shard_map/ppermute | solution.py:48
  74.5 10.0 %qkv.1 = (bf16[3,512,384]{2,1,0:T(8,128)(2,1)}, bf16[3,512,384]{2,1,0:T(8,128)(2,1)}, bf16[3,512,384]{2,1,0:T(8,128)(2,1)}, bf16[3,512,768]{2,1,0:T(8,128)(2,1)}...) custom-call(s32[2]{0:T(128)} %pad_add_fusion.1.meta, s32[16]{0:T(128)} %broadcast_xor_fusion.pos, ...), custom_call_target="tpu_custom_call" | custom-call | tf_op jit(solution)/shard_map/qkv/pallas_call | solution.py:533
  84.6 24.7 %attend.1 = (bf16[3,256,384]{2,1,0:T(8,128)(2,1)}, bf16[3,256,384]{2,1,0:T(8,128)(2,1)}, bf16[3,3,2,512,512]{4,3,2,1,0:T(8,128)(2,1)}, f32[3,512,384]{2,1,0:T(8,128)}) custom-call(s32[2]{0:T(128)} %pad_add_fusion.1.meta, bf16[3,512,384]{2,1,0:T(8,128)(2,1)} %get-tuple-element.58.q_ref, bf16[3,512,384]{2,1,0:T(8,128)(2,1)} %get-tuple-element.59.k_ref, ...), custom_call_target="tpu_custom_call" | custom-call | tf_op jit(solution)/shard_map/attend/pallas_call | solution.py:557
  119.3 6.6 %middle.1 = (f32[3,256,768]{2,1,0:T(8,128)}, bf16[3,256,768]{2,1,0:T(8,128)(2,1)}, bf16[2,768,384]{2,1,0:T(8,128)(2,1)}) custom-call(s32[2]{0:T(128)} %pad_add_fusion.1.meta, s32[16]{0:T(128)} %broadcast_xor_fusion.pos, bf16[3,256,768]{2,1,0:T(8,128)(2,1)} %x_ref.3, bf16[3,256,384]{2,1,0:T(8,128)(2,1)} %get-tuple-element.62.own_ref, ...), custom_call_target="tpu_custom_call" | custom-call | tf_op jit(solution)/shard_map/middle/pallas_call | solution.py:577
  126.0 5.2 %collective-permute-done.24 = bf16[2,96,768]{2,1,0:T(8,128)(2,1)S(1)} collective-permute-done((bf16[2,96,768]{2,1,0:T(8,128)(2,1)S(1)}, bf16[2,96,768]{2,1,0:T(8,128)(2,1)S(1)}, u32[]{:S(2)}, u32[]{:S(2)}) %collective-permute-start.24) | collective-permute-done | bytes 294944 | tf_op jit(solution)/shard_map/ppermute | solution.py:48
  134.7 8.8 %collective-permute-done.20.rest_6_ = bf16[4,48,1024]{2,1,0:T(8,128)(2,1)S(1)} collective-permute-done((bf16[4,48,1024]{2,1,0:T(8,128)(2,1)S(1)}, bf16[4,48,1024]{2,1,0:T(8,128)(2,1)S(1)}, u32[]{:S(2)}, u32[]{:S(2)}) %collective-permute-start.20) | collective-permute-done | bytes 393248 | tf_op jit(solution)/shard_map/ppermute | solution.py:48
  149.0 10.9 %collective-permute-done.25.rest_1_ = bf16[4,96,384]{2,1,0:T(8,128)(2,1)S(1)} collective-permute-done((bf16[4,96,384]{2,1,0:T(8,128)(2,1)S(1)}, bf16[4,96,384]{2,1,0:T(8,128)(2,1)S(1)}, u32[]{:S(2)}, u32[]{:S(2)}) %collective-permute-start.25) | collective-permute-done | bytes 294944 | tf_op jit(solution)/shard_map/ppermute | solution.py:48
  164.5 12.6 %hidden.1 = (bf16[3,512,1536]{2,1,0:T(8,128)(2,1)}, bf16[3,512,1536]{2,1,0:T(8,128)(2,1)}, bf16[768,1536]{1,0:T(8,128)(2,1)}) custom-call(s32[16]{0:T(128)} %broadcast_xor_fusion.pos, bf16[3,256,768]{2,1,0:T(8,128)(2,1)} %get-tuple-element.66.own_ref.rest_0_, bf16[3,256,768]{2,1,0:T(8,128)(2,1)} %copy-done.5, bf16[4,48,896]{2,1,0:T(8,128)(2,1)} %copy-done.10, ...), custom_call_target="tpu_custom_call" | custom-call | tf_op jit(solution)/shard_map/hidden/pallas_call | solution.py:590
  177.0 5.0 %fusion.25 = (bf16[3,256,1536]{2,1,0:T(8,128)(2,1)}, bf16[3,256,1536]{2,1,0:T(8,128)(2,1)}) fusion(bf16[3,512,1536]{2,1,0:T(8,128)(2,1)} %get-tuple-element.67.act_ref), kind=kLoop, calls=%fused_computation.138 | loop fusion | bytes 9437184 | tf_op jit(solution)/shard_map/slice | solution.py:654
  183.6 14.7 %ffn_back.1 = (bf16[3,512,1536]{2,1,0:T(8,128)(2,1)}, f32[3,256,768]{2,1,0:T(8,128)}, bf16[3,256,768]{2,1,0:T(8,128)(2,1)}, bf16[1536,768]{1,0:T(8,128)(2,1)}) custom-call(s32[16]{0:T(128)} %broadcast_xor_fusion.pos, bf16[3,256,768]{2,1,0:T(8,128)(2,1)} %rest_2_.1, bf16[3,256,768]{2,1,0:T(8,128)(2,1)} %copy-done.3, ...), custom_call_target="tpu_custom_call" | custom-call | tf_op jit(solution)/shard_map/ffn_back/pallas_call | solution.py:659
  198.3 7.5 %ffn_out.1 = (f32[3,256,768]{2,1,0:T(8,128)}, bf16[3,256,768]{2,1,0:T(8,128)(2,1)}) custom-call(bf16[3,512,1536]{2,1,0:T(8,128)(2,1)} %get-tuple-element.67.act_ref, bf16[1536,768]{1,0:T(8,128)(2,1)} %get-tuple-element.70.w), custom_call_target="tpu_custom_call" | custom-call | tf_op jit(solution)/shard_map/ffn_out/pallas_call | solution.py:682
  205.8 8.5 %grad_ffn_out.1 = (bf16[2,4,96,384]{3,2,1,0:T(8,128)(2,1)}, bf16[2,4,96,384]{3,2,1,0:T(8,128)(2,1)}, bf16[2,4,96,384]{3,2,1,0:T(8,128)(2,1)}, bf16[2,4,96,384]{3,2,1,0:T(8,128)(2,1)}) custom-call(s32[2]{0:T(128)} %pad_add_fusion.1.meta, bf16[3,256,1536]{2,1,0:T(8,128)(2,1)} %get-tuple-element.114.rest_0_, bf16[3,256,1536]{2,1,0:T(8,128)(2,1)} %get-tuple-element.113.rest_1_, ...), custom_call_target="tpu_custom_call" | custom-call | tf_op jit(solution)/shard_map/grad_ffn_out/pallas_call | solution.py:638
  219.7 8.6 %grad_ffn_in.1 = (bf16[2,4,48,768]{3,2,1,0:T(8,128)(2,1)}, bf16[2,4,48,768]{3,2,1,0:T(8,128)(2,1)}, bf16[2,4,48,768]{3,2,1,0:T(8,128)(2,1)}, bf16[2,4,48,768]{3,2,1,0:T(8,128)(2,1)}) custom-call(s32[2]{0:T(128)} %pad_add_fusion.1.meta, bf16[3,256,768]{2,1,0:T(8,128)(2,1)} %get-tuple-element.66.own_ref.rest_0_, bf16[3,256,768]{2,1,0:T(8,128)(2,1)} %copy-done.5, ...), custom_call_target="tpu_custom_call" | custom-call | tf_op jit(solution)/shard_map/grad_ffn_in/pallas_call | solution.py:638
  231.7 12.0 %collective-permute-done.50 = bf16[2,4,48,768]{3,2,1,0:T(8,128)(2,1)S(1)} collective-permute-done((bf16[2,4,48,768]{3,2,1,0:T(8,128)(2,1)}, bf16[2,4,48,768]{3,2,1,0:T(8,128)(2,1)S(1)}, u32[]{:S(2)}, u32[]{:S(2)}) %collective-permute-start.50) | collective-permute-done | bytes 589856 | tf_op jit(solution)/shard_map/ppermute | solution.py:48
  246.8 5.2 %collective-permute-done.58 = bf16[4,96,384]{2,1,0:T(8,128)(2,1)S(1)} collective-permute-done((bf16[4,96,384]{2,1,0:T(8,128)(2,1)S(1)}, bf16[4,96,384]{2,1,0:T(8,128)(2,1)S(1)}, u32[]{:S(2)}, u32[]{:S(2)}) %collective-permute-start.58) | collective-permute-done | bytes 294944 | tf_op jit(solution)/shard_map/ppermute | solution.py:48
  259.6 15.4 %collective-permute-done.61 = bf16[2,96,768]{2,1,0:T(8,128)(2,1)} collective-permute-done((bf16[2,96,768]{2,1,0:T(8,128)(2,1)}, bf16[2,96,768]{2,1,0:T(8,128)(2,1)}, u32[]{:S(2)}, u32[]{:S(2)}) %collective-permute-start.61) | collective-permute-done | bytes 294944 | tf_op jit(solution)/shard_map/ppermute | solution.py:48
  277.7 7.2 %middle_back.1 = (f32[3,256,768]{2,1,0:T(8,128)}, bf16[3,256,768]{2,1,0:T(8,128)(2,1)}, bf16[3,256,384]{2,1,0:T(8,128)(2,1)}, bf16[3,256,384]{2,1,0:T(8,128)(2,1)}) custom-call(s32[2]{0:T(128)} %pad_add_fusion.1.meta, bf16[3,256,768]{2,1,0:T(8,128)(2,1)} %rest_2_.1, f32[3,256,768]{2,1,0:T(8,128)} %get-tuple-element.65.mid_ref, ...), custom_call_target="tpu_custom_call" | custom-call | tf_op jit(solution)/shard_map/middle_back/pallas_call | solution.py:693
  304.7 34.6 %attend_back.1 = (bf16[3,512,384]{2,1,0:T(8,128)(2,1)}, bf16[3,512,384]{2,1,0:T(8,128)(2,1)}, bf16[3,512,384]{2,1,0:T(8,128)(2,1)}, f32[3,2,1024]{2,1,0:T(2,128)}) custom-call(s32[2]{0:T(128)} %pad_add_fusion.1.meta, bf16[3,512,384]{2,1,0:T(8,128)(2,1)} %get-tuple-element.58.q_ref, bf16[3,512,384]{2,1,0:T(8,128)(2,1)} %get-tuple-element.59.k_ref, ...), custom_call_target="tpu_custom_call" | custom-call | tf_op jit(solution)/shard_map/attend_back/pallas_call | solution.py:730
  340.7 7.5 %input_grad.1 = (f32[3,256,768]{2,1,0:T(8,128)}, bf16[3,256,768]{2,1,0:T(8,128)(2,1)}) custom-call(s32[2]{0:T(128)} %pad_add_fusion.1.meta, bf16[3,512,384]{2,1,0:T(8,128)(2,1)} %get-tuple-element.81.dq_ref, bf16[3,512,384]{2,1,0:T(8,128)(2,1)} %get-tuple-element.82.dk_ref, bf16[3,512,384]{2,1,0:T(8,128)(2,1)} %get-tuple-element.83.dv_ref, ...), custom_call_target="tpu_custom_call" | custom-call | tf_op jit(solution)/shard_map/input_grad/pallas_call | solution.py:769
  348.2 9.8 %grad_qkv.1 = (bf16[2,4,48,640]{3,2,1,0:T(8,128)(2,1)}, bf16[2,4,48,640]{3,2,1,0:T(8,128)(2,1)}, bf16[2,4,48,640]{3,2,1,0:T(8,128)(2,1)}, bf16[2,4,48,640]{3,2,1,0:T(8,128)(2,1)}) custom-call(s32[2]{0:T(128)} %pad_add_fusion.1.meta, bf16[3,512,768]{2,1,0:T(8,128)(2,1)} %get-tuple-element.87.norm_ref, bf16[3,512,384]{2,1,0:T(8,128)(2,1)} %get-tuple-element.81.dq_ref, ...), custom_call_target="tpu_custom_call" | custom-call | tf_op jit(solution)/shard_map/grad_qkv/pallas_call | solution.py:752
  362.3 10.7 %collective-permute-done.44 = bf16[4,48,128]{2,1,0:T(8,128)(2,1)S(1)} collective-permute-done((bf16[4,48,128]{2,1,0:T(8,128)(2,1)S(1)}, bf16[4,48,128]{2,1,0:T(8,128)(2,1)S(1)}, u32[]{:S(2)}, u32[]{:S(2)}) %collective-permute-start.44) | collective-permute-done | bytes 49184 | tf_op jit(solution)/shard_map/ppermute | solution.py:48
  384.6 9.2 %collective-permute-done.39 = bf16[2,48,1280]{2,1,0:T(8,128)(2,1)S(1)} collective-permute-done((bf16[2,48,1280]{2,1,0:T(8,128)(2,1)S(1)}, bf16[2,48,1280]{2,1,0:T(8,128)(2,1)S(1)}, u32[]{:S(2)}, u32[]{:S(2)}) %collective-permute-start.39) | collective-permute-done | bytes 245792 | tf_op jit(solution)/shard_map/ppermute | solution.py:48
  404.8 5.2 %last.1 = bf16[3,256,768]{2,1,0:T(8,128)(2,1)} custom-call(bf16[3,256,768]{2,1,0:T(8,128)(2,1)} %x_ref.3, f32[3,256,768]{2,1,0:T(8,128)} %get-tuple-element.76.gm_ref, f32[3,256,768]{2,1,0:T(8,128)} %get-tuple-element.85.own_ref, bf16[3,256,768]{2,1,0:T(8,128)(2,1)} %copy-done.11, f32[8,768]{1,0:T(8,128)} %get-tuple-element.64.misc), custom_call_target="tpu_custom_call" | custom-call | tf_op jit(solution)/shard_map/last/pallas_call | solution.py:778
  (335 shorter events, 146.1 us)
Async XLA Ops:
  13.0 23.2 %collective-permute-start.3 = (bf16[2,48,1280]{2,1,0:T(8,128)(2,1)S(1)}, bf16[2,48,1280]{2,1,0:T(8,128)(2,1)S(1)}, u32[]{:S(2)}, u32[]{:S(2)}) collective-permute-start(bf16[2,48,1280]{2,1,0:T(8,128)(2,1)S(1)} %pad_maximum_fusion.12), channel_id=1, source_target_pairs={{0,16},{2,18},{4,20},{6,22},{8,24},{10,26},{12,28},{14,30},{16,0},... | collective-permute-start | bytes 737288 | tf_op jit(solution)/shard_map/ppermute | solution.py:48
  16.2 57.3 %collective-permute-start = (bf16[3,256,768]{2,1,0:T(8,128)(2,1)S(1)}, bf16[3,256,768]{2,1,0:T(8,128)(2,1)S(1)}, u32[]{:S(2)}, u32[]{:S(2)}) collective-permute-start(bf16[3,256,768]{2,1,0:T(8,128)(2,1)S(1)} %copy-done.1), channel_id=1, source_target_pairs={{0,1},{1,0},{2,3},{3,2},{4,5},{5,4},{6,7},{7,6},{8,9},{9,8},{10,11... | collective-permute-start | bytes 3538952 | tf_op jit(solution)/shard_map/ppermute | solution.py:85
  19.3 22.8 %collective-permute-start.13 = (bf16[2,48,1920]{2,1,0:T(8,128)(2,1)S(1)}, bf16[2,48,1920]{2,1,0:T(8,128)(2,1)S(1)}, u32[]{:S(2)}, u32[]{:S(2)}) collective-permute-start(bf16[2,48,1920]{2,1,0:T(8,128)(2,1)S(1)} %pad_maximum_fusion.6), channel_id=1, source_target_pairs={{0,16},{2,18},{4,20},{6,22},{8,24},{10,26},{12,28},{14,30},{16,0},... | collective-permute-start | bytes 1105928 | tf_op jit(solution)/shard_map/ppermute | solution.py:48
  45.7 16.5 %collective-permute-start.15 = (bf16[4,48,896]{2,1,0:T(8,128)(2,1)S(1)}, bf16[4,48,896]{2,1,0:T(8,128)(2,1)}, u32[]{:S(2)}, u32[]{:S(2)}) collective-permute-start(bf16[4,48,896]{2,1,0:T(8,128)(2,1)S(1)} %pad_maximum_fusion.7.rest_0_), channel_id=1, source_target_pairs={{0,4},{2,6},{4,0},{6,2},{8,12},{10,14},{12,8},{14,10},{16,20},{18,... | collective-permute-start | bytes 1032200 | tf_op jit(solution)/shard_map/ppermute | solution.py:48
  53.3 56.0 %collective-permute-start.16 = (bf16[4,48,896]{2,1,0:T(8,128)(2,1)}, bf16[4,48,896]{2,1,0:T(8,128)(2,1)S(1)}, u32[]{:S(2)}, u32[]{:S(2)}) collective-permute-start(bf16[4,48,896]{2,1,0:T(8,128)(2,1)} %collective-permute-done.14.rest_1_), channel_id=1, source_target_pairs={{0,4},{2,6},{4,0},{6,2},{8,12},{10,14},{12,8},{14,10},{16,20},{18,... | collective-permute-start | bytes 1032200 | tf_op jit(solution)/shard_map/ppermute | solution.py:48
  125.9 37.5 %collective-permute-start.18 = (bf16[3,256,768]{2,1,0:T(8,128)(2,1)}, bf16[3,256,768]{2,1,0:T(8,128)(2,1)S(1)}, u32[]{:S(2)}, u32[]{:S(2)}) collective-permute-start(bf16[3,256,768]{2,1,0:T(8,128)(2,1)} %get-tuple-element.66.own_ref.rest_0_), channel_id=1, source_target_pairs={{0,1},{1,0},{2,3},{3,2},{4,5},{5,4},{6,7},{7,6},{8,9},{9,8},{10,11... | collective-permute-start | bytes 3538952 | tf_op jit(solution)/shard_map/ppermute | solution.py:85
  133.6 48.6 %collective-permute-start.22 = (bf16[3,256,768]{2,1,0:T(8,128)(2,1)S(1)}, bf16[3,256,768]{2,1,0:T(8,128)(2,1)S(1)}, u32[]{:S(2)}, u32[]{:S(2)}) collective-permute-start(bf16[3,256,768]{2,1,0:T(8,128)(2,1)S(1)} %copy-done), channel_id=1, source_target_pairs={{0,1},{1,0},{2,3},{3,2},{4,5},{5,4},{6,7},{7,6},{8,9},{9,8},{10,11... | collective-permute-start | bytes 3538952 | tf_op jit(solution)/shard_map/ppermute | solution.py:85
  133.6 27.4 %collective-permute-start.19 = (bf16[4,48,1024]{2,1,0:T(8,128)(2,1)S(1)}, bf16[4,48,1024]{2,1,0:T(8,128)(2,1)S(1)}, u32[]{:S(2)}, u32[]{:S(2)}) collective-permute-start(bf16[4,48,1024]{2,1,0:T(8,128)(2,1)S(1)} %pad_maximum_fusion.4.rest_4_), channel_id=1, source_target_pairs={{0,2},{2,0},{4,6},{6,4},{8,10},{10,8},{12,14},{14,12},{16,18},{18,... | collective-permute-start | bytes 1179656 | tf_op jit(solution)/shard_map/ppermute | solution.py:48
  143.5 19.0 %collective-permute-start.21 = (bf16[4,48,1024]{2,1,0:T(8,128)(2,1)S(1)}, bf16[4,48,1024]{2,1,0:T(8,128)(2,1)S(1)}, u32[]{:S(2)}, u32[]{:S(2)}) collective-permute-start(bf16[4,48,1024]{2,1,0:T(8,128)(2,1)S(1)} %collective-permute-done.20.rest_6_), channel_id=1, source_target_pairs={{0,2},{2,0},{4,6},{6,4},{8,10},{10,8},{12,14},{14,12},{16,18},{18,... | collective-permute-start | bytes 1179656 | tf_op jit(solution)/shard_map/ppermute | solution.py:48
  159.9 22.2 %collective-permute-start.28 = (bf16[4,96,384]{2,1,0:T(8,128)(2,1)S(1)}, bf16[4,96,384]{2,1,0:T(8,128)(2,1)S(1)}, u32[]{:S(2)}, u32[]{:S(2)}) collective-permute-start(bf16[4,96,384]{2,1,0:T(8,128)(2,1)S(1)} %get-tuple-element.117.rest_4_), channel_id=1, source_target_pairs={{0,2},{2,0},{4,6},{6,4},{8,10},{10,8},{12,14},{14,12},{16,18},{18,... | collective-permute-start | bytes 884744 | tf_op jit(solution)/shard_map/ppermute | solution.py:48
  161.0 21.1 %collective-permute-start.26 = (bf16[4,96,384]{2,1,0:T(8,128)(2,1)S(1)}, bf16[4,96,384]{2,1,0:T(8,128)(2,1)S(1)}, u32[]{:S(2)}, u32[]{:S(2)}) collective-permute-start(bf16[4,96,384]{2,1,0:T(8,128)(2,1)S(1)} %get-tuple-element.118.rest_0_), channel_id=1, source_target_pairs={{0,4},{2,6},{4,0},{6,2},{8,12},{10,14},{12,8},{14,10},{16,20},{18,... | collective-permute-start | bytes 884744 | tf_op jit(solution)/shard_map/ppermute | solution.py:48
  162.5 19.6 %collective-permute-start.30 = (bf16[4,96,384]{2,1,0:T(8,128)(2,1)S(1)}, bf16[4,96,384]{2,1,0:T(8,128)(2,1)S(1)}, u32[]{:S(2)}, u32[]{:S(2)}) collective-permute-start(bf16[4,96,384]{2,1,0:T(8,128)(2,1)S(1)} %collective-permute-done.29.rest_6_), channel_id=1, source_target_pairs={{0,2},{2,0},{4,6},{6,4},{8,10},{10,8},{12,14},{14,12},{16,18},{18,... | collective-permute-start | bytes 884744 | tf_op jit(solution)/shard_map/ppermute | solution.py:48
  163.5 18.7 %collective-permute-start.27 = (bf16[4,96,384]{2,1,0:T(8,128)(2,1)S(1)}, bf16[4,96,384]{2,1,0:T(8,128)(2,1)S(1)}, u32[]{:S(2)}, u32[]{:S(2)}) collective-permute-start(bf16[4,96,384]{2,1,0:T(8,128)(2,1)S(1)} %collective-permute-done.25.rest_1_), channel_id=1, source_target_pairs={{0,4},{2,6},{4,0},{6,2},{8,12},{10,14},{12,8},{14,10},{16,20},{18,... | collective-permute-start | bytes 884744 | tf_op jit(solution)/shard_map/ppermute | solution.py:48
  216.5 76.2 %collective-permute-start.31 = (bf16[3,256,768]{2,1,0:T(8,128)(2,1)}, bf16[3,256,768]{2,1,0:T(8,128)(2,1)S(1)}, u32[]{:S(2)}, u32[]{:S(2)}) collective-permute-start(bf16[3,256,768]{2,1,0:T(8,128)(2,1)} %get-tuple-element.72), channel_id=1, source_target_pairs={{0,1},{1,0},{2,3},{3,2},{4,5},{5,4},{6,7},{7,6},{8,9},{9,8},{10,11... | collective-permute-start | bytes 3538952 | tf_op jit(solution)/shard_map/ppermute | solution.py:85
  216.5 60.2 %collective-permute-start.32 = (bf16[3,256,768]{2,1,0:T(8,128)(2,1)}, bf16[3,256,768]{2,1,0:T(8,128)(2,1)S(1)}, u32[]{:S(2)}, u32[]{:S(2)}) collective-permute-start(bf16[3,256,768]{2,1,0:T(8,128)(2,1)} %get-tuple-element.74), channel_id=1, source_target_pairs={{0,1},{1,0},{2,3},{3,2},{4,5},{5,4},{6,7},{7,6},{8,9},{9,8},{10,11... | collective-permute-start | bytes 3538952 | tf_op jit(solution)/shard_map/ppermute | solution.py:85
  229.2 16.4 %collective-permute-start.52 = (bf16[2,4,48,768]{3,2,1,0:T(8,128)(2,1)}, bf16[2,4,48,768]{3,2,1,0:T(8,128)(2,1)S(1)}, u32[]{:S(2)}, u32[]{:S(2)}) collective-permute-start(bf16[2,4,48,768]{3,2,1,0:T(8,128)(2,1)} %get-tuple-element.100), channel_id=1, source_target_pairs={{0,2},{2,0},{4,6},{6,4},{8,10},{10,8},{12,14},{14,12},{16,18},{18,... | collective-permute-start | bytes 1769480 | tf_op jit(solution)/shard_map/ppermute | solution.py:48
  230.4 21.6 %collective-permute-start.58 = (bf16[4,96,384]{2,1,0:T(8,128)(2,1)S(1)}, bf16[4,96,384]{2,1,0:T(8,128)(2,1)S(1)}, u32[]{:S(2)}, u32[]{:S(2)}) collective-permute-start(bf16[4,96,384]{2,1,0:T(8,128)(2,1)S(1)} %slice_bitcast_fusion.3), channel_id=1, source_target_pairs={{0,2},{2,0},{4,6},{6,4},{8,10},{10,8},{12,14},{14,12},{16,18},{18,... | collective-permute-start | bytes 884744 | tf_op jit(solution)/shard_map/ppermute | solution.py:48
  254.0 21.0 %collective-permute-start.61 = (bf16[2,96,768]{2,1,0:T(8,128)(2,1)}, bf16[2,96,768]{2,1,0:T(8,128)(2,1)}, u32[]{:S(2)}, u32[]{:S(2)}) collective-permute-start(bf16[2,96,768]{2,1,0:T(8,128)(2,1)} %pad_maximum_fusion.8), channel_id=1, source_target_pairs={{0,16},{2,18},{4,20},{6,22},{8,24},{10,26},{12,28},{14,30},{16,0},... | collective-permute-start | bytes 884744 | tf_op jit(solution)/shard_map/ppermute | solution.py:48
  259.5 29.9 %collective-permute-start.54 = (bf16[2,48,1536]{2,1,0:T(8,128)(2,1)}, bf16[2,48,1536]{2,1,0:T(8,128)(2,1)}, u32[]{:S(2)}, u32[]{:S(2)}) collective-permute-start(bf16[2,48,1536]{2,1,0:T(8,128)(2,1)} %pad_maximum_fusion.9), channel_id=1, source_target_pairs={{0,16},{2,18},{4,20},{6,22},{8,24},{10,26},{12,28},{14,30},{16,0},... | collective-permute-start | bytes 884744 | tf_op jit(solution)/shard_map/ppermute | solution.py:48
  276.7 20.1 %collective-permute-start.62 = (bf16[1,96,768]{2,1,0:T(8,128)(2,1)}, bf16[1,96,768]{2,1,0:T(8,128)(2,1)}, u32[]{:S(2)}, u32[]{:S(2)}) collective-permute-start(bf16[1,96,768]{2,1,0:T(8,128)(2,1)} %slice.303), channel_id=1, source_target_pairs={{0,8},{2,10},{4,12},{6,14},{8,0},{10,2},{12,4},{14,6},{16,24},{18,... | collective-permute-start | bytes 442376 | tf_op jit(solution)/shard_map/ppermute | solution.py:48
  301.7 58.4 %collective-permute-start.43 = (bf16[2,4,48,128]{3,2,1,0:T(8,128)(2,1)S(1)}, bf16[2,4,48,128]{3,2,1,0:T(8,128)(2,1)S(1)}, u32[]{:S(2)}, u32[]{:S(2)}) collective-permute-start(bf16[2,4,48,128]{3,2,1,0:T(8,128)(2,1)S(1)} %slice_bitcast_fusion.19), channel_id=1, source_target_pairs={{0,4},{2,6},{4,0},{6,2},{8,12},{10,14},{12,8},{14,10},{16,20},{18,... | collective-permute-start | bytes 294920 | tf_op jit(solution)/shard_map/ppermute | solution.py:48
  302.9 58.3 %collective-permute-start.45 = (bf16[2,4,48,256]{3,2,0,1:T(8,128)(2,1)S(1)}, bf16[2,4,48,256]{3,2,0,1:T(8,128)(2,1)S(1)}, u32[]{:S(2)}, u32[]{:S(2)}) collective-permute-start(bf16[2,4,48,256]{3,2,0,1:T(8,128)(2,1)S(1)} %slice_bitcast_fusion.13), channel_id=1, source_target_pairs={{0,2},{2,0},{4,6},{6,4},{8,10},{10,8},{12,14},{14,12},{16,18},{18,... | collective-permute-start | bytes 589832 | tf_op jit(solution)/shard_map/ppermute | solution.py:48
  359.0 16.5 %collective-permute-start.37 = (bf16[2,4,48,640]{3,2,1,0:T(8,128)(2,1)}, bf16[2,4,48,640]{3,2,1,0:T(8,128)(2,1)S(1)}, u32[]{:S(2)}, u32[]{:S(2)}) collective-permute-start(bf16[2,4,48,640]{3,2,1,0:T(8,128)(2,1)} %get-tuple-element.92), channel_id=1, source_target_pairs={{0,2},{2,0},{4,6},{6,4},{8,10},{10,8},{12,14},{14,12},{16,18},{18,... | collective-permute-start | bytes 1474568 | tf_op jit(solution)/shard_map/ppermute | solution.py:48
  360.1 43.7 %collective-permute-start.34 = (bf16[3,256,768]{2,1,0:T(8,128)(2,1)S(1)}, bf16[3,256,768]{2,1,0:T(8,128)(2,1)S(1)}, u32[]{:S(2)}, u32[]{:S(2)}) collective-permute-start(bf16[3,256,768]{2,1,0:T(8,128)(2,1)S(1)} %copy-done.54), channel_id=1, source_target_pairs={{0,1},{1,0},{2,3},{3,2},{4,5},{5,4},{6,7},{7,6},{8,9},{9,8},{10,11... | collective-permute-start | bytes 3538952 | tf_op jit(solution)/shard_map/ppermute | solution.py:85
  (95 other events, 897.1 us)

commit v2 on v1

--- a/solution.py
+++ b/solution.py
@@ -28,8 +28,18 @@
     return pl.BlockSpec(shape, lambda *_: zeros)
 
 
-def params(**extra):
-    return pltpu.CompilerParams(vmem_limit_bytes=56 * 1024 * 1024, **extra)
+def params(mib=16):
+    return pltpu.CompilerParams(vmem_limit_bytes=mib * 1024 * 1024)
+
+
+MICROS = {
+    "qkv": 10, "attend": 25, "middle": 7, "hidden": 12, "grad_ffn_out": 9, "grad_ffn_in": 9, "ffn_back": 15, "ffn_out": 8,
+    "middle_back": 7, "grad_output": 4, "attend_back": 35, "grad_qkv": 10, "input_grad": 8, "last": 5,
+}
+
+
+def cost(name):
+    return pl.CostEstimate(flops=int(MICROS[name] * 1.15e9), bytes_accessed=0, transcendentals=0)
 
 
 def nn(a, b):
@@ -48,49 +58,102 @@
     return lax.ppermute(x, axis, [(i, i ^ bit) for i in range(count)])
 
 
-def gather_pieces(block, cut, dp):
-    have = block[None]
-    bit = 4
-    while bit < dp:
-        have = jnp.concatenate([have, flip(have, "dp", bit, dp)], axis=0)
-        bit *= 2
-    left, right = have[..., :cut], have[..., cut:]
-    left_x = flip(left, "dp", 1, dp)
-    right_y = flip(right, "dp", 2, dp)
-    left_y = flip(left, "dp", 2, dp)
-    right_x = flip(right, "dp", 1, dp)
-    left_xy = flip(left_x, "dp", 2, dp)
-    right_xy = flip(right_y, "dp", 1, dp)
-    return [left, left_x, left_y, left_xy], [right, right_x, right_y, right_xy]
-
-
-def scatter_pieces(left_send, left_keep, right_send, right_keep, dp):
-    def add(a, b):
-        return (a.astype(F32) + b.astype(F32)).astype(BF)
-
-    left = add(left_keep, flip(left_send, "dp", 2, dp))
-    right = add(right_keep, flip(right_send, "dp", 1, dp))
-    left = add(left[0], flip(left[1], "dp", 1, dp))
-    right = add(right[0], flip(right[1], "dp", 2, dp))
-    have = jnp.concatenate([left, right], axis=-1)
-    bit = dp // 2
-    while bit >= 4:
-        half = have.shape[0] // 2
-        have = add(have[:half], flip(have[half:], "dp", bit, dp))
-        bit //= 2
-    return have[0]
+def after(values, *others):
+    return lax.optimization_barrier((values, others))[0]
+
+
+def meet(values, *fields):
+    held = [[getattr(owner, name) for name in names.split()] for owner, names in fields]
+    values, held = lax.optimization_barrier((values, held))
+    for (owner, names), got in zip(fields, held):
+        for name, value in zip(names.split(), got):
+            setattr(owner, name, value)
+    return values
+
+
+def bit_groups(dp):
+    bits, groups = dp.bit_length() - 3, []
+    at = 2
+    while bits > 0:
+        groups.append((1 << at, 1 << min(bits, 2)))
+        at, bits = at + 2, bits - 2
+    return groups
+
+
+class Gather:
+    def __init__(self, block, cut, dp):
+        self.have, self.cut, self.dp = block[None], cut, dp
+
+    def high(self):
+        for bit, size in bit_groups(self.dp):
+            got = [flip(self.have, "dp", bit * k, self.dp) for k in range(1, size)]
+            self.have, self.got = jnp.concatenate([self.have] + got, axis=0), got
+
+    def first(self):
+        self.left, self.right = self.have[..., : self.cut], self.have[..., self.cut :]
+        self.left_x = flip(self.left, "dp", 1, self.dp)
+        self.right_y = flip(self.right, "dp", 2, self.dp)
+
+    def second(self):
+        self.left = jnp.concatenate([self.left, self.left_x], axis=0)
+        self.right = jnp.concatenate([self.right, self.right_y], axis=0)
+        self.left_far = flip(self.left, "dp", 2, self.dp)
+        self.right_far = flip(self.right, "dp", 1, self.dp)
+
+    def pieces(self):
+        return [self.left, self.left_far], [self.right, self.right_far]
+
+
+class Scatter:
+    def __init__(self, parts, dp):
+        self.left_send, self.left_keep, self.right_send, self.right_keep = parts
+        self.dp, self.groups = dp, bit_groups(dp)
+
+    @staticmethod
+    def add(*terms):
+        return sum(x.astype(F32) for x in terms).astype(BF)
+
+    def first(self):
+        self.left_got = flip(self.left_send, "dp", 2, self.dp)
+        self.right_got = flip(self.right_send, "dp", 1, self.dp)
+
+    def second(self):
+        self.left = self.add(self.left_keep, self.left_got)
+        self.right = self.add(self.right_keep, self.right_got)
+        self.left_got = flip(self.left[1], "dp", 1, self.dp)
+        self.right_got = flip(self.right[1], "dp", 2, self.dp)
+
+    def join(self):
+        left = self.add(self.left[0], self.left_got)
+        right = self.add(self.right[0], self.right_got)
+        self.have = jnp.concatenate([left, right], axis=-1)
+
+    def send(self):
+        bit, size = self.groups.pop()
+        parts = self.have.reshape((size, -1) + self.have.shape[1:])
+        self.keep = parts[0]
+        self.got = [flip(parts[k], "dp", bit * k, self.dp) for k in range(1, size)]
+
+    def take(self):
+        self.have = self.add(self.keep, *self.got)
+
+    def rest(self):
+        while self.groups:
+            self.send()
+            self.take()
+        return self.have[0]
 
 
 def other_core(x):
     return lax.ppermute(x, "seq", [(0, 1), (1, 0)])
 
 
-def start_blocks(refs, pos, rows, dst, cols, sems):
+def start_blocks(refs, pos, side, rows, dst, cols, sems):
     copies = []
     at = 0
     for ref in refs:
         for b in range(ref.shape[0]):
-            row = pl.multiple_of(pos[at] * rows, rows)
+            row = pl.multiple_of(pos[side, at] * rows, rows)
             src = ref.at[b] if cols is None else ref.at[b, :, pl.ds(*cols)]
             copies.append(pltpu.make_async_copy(src, dst.at[pl.ds(row, rows)], sems.at[at]))
             at += 1
@@ -108,8 +171,8 @@
 
     @pl.when(pl.program_id(0) == 0)
     def _():
-        copies = start_blocks(left, pos, rows, wl, None, sem_l)
-        copies += start_blocks(right, pos, rows, wr, None, sem_r)
+        copies = start_blocks(left, pos, 0, rows, wl, None, sem_l)
+        copies += start_blocks(right, pos, 1, rows, wr, None, sem_r)
         for copy in copies:
             copy.wait()
         w[:, :cut] = wl[...]
@@ -141,11 +204,12 @@
     return (lane < HEAD_DIM) if which == 0 else (lane >= HEAD_DIM)
 
 
-def attend_kernel(meta, q_ref, k_ref, v_ref, mask_ref, peroff, own_ref, oth_ref, e_ref, inv_ref, grid, ctx):
+def attend_kernel(meta, q_ref, k_ref, v_ref, mask_ref, peroff, own_ref, oth_ref, e_ref, inv_ref, grid, ctx, table):
     s = meta[0]
     hp = pl.program_id(0)
     length = q_ref.shape[1]
     step = LANES
+    rows = step // 2
     span = grid.shape[-1]
 
     @pl.when(pl.program_id(1) == 0)
@@ -159,21 +223,17 @@
     zero = jnp.zeros((), BF)
     one = jnp.ones((), BF)
     first = lane_half((length, LANES), 0)
+    for hh in range(2):
+        table[hh] = nt(jnp.where(first if hh == 0 else ~first, q, zero), k)
     sums = []
     for hh in range(2):
-        keep = first if hh == 0 else ~first
-        q_head = jnp.where(keep, q, zero)
-        v_head = jnp.where(keep, v, one)
-        parts = []
-        for a in range(length // step):
-            base = length - step - a * step
-            scores = nt(q_head[a * step : (a + 1) * step], k)
-            scores = scores + grid[hh, :, base : base + length] + mask
+        for at in range(0, length, rows):
+            base, within = length - step - at // step * step, at % step
+            bias = grid[hh, within : within + rows, base : base + length]
+            scores = table[hh, at : at + rows] + (bias + mask)
             top = jnp.max(scores, axis=-1, keepdims=True)
-            low = jnp.exp(scores - top).astype(BF)
-            e_ref[0, 0, hh, a * step : (a + 1) * step, :] = low
-            parts.append(nn(low, v_head))
-        sums.append(jnp.concatenate(parts, axis=0))
+            e_ref[0, 0, hh, at : at + rows, :] = jnp.exp(scores - top).astype(BF)
+        sums.append(nn(e_ref[0, 0, hh], jnp.where(first if hh == 0 else ~first, v, one)))
     num = jnp.where(first, sums[0], sums[1])
     den = pltpu.roll(jnp.where(first, sums[1], sums[0]), HEAD_DIM, 1)
     inv = 1.0 / den
@@ -192,8 +252,8 @@
 
     @pl.when(pl.program_id(0) == 0)
     def _():
-        copies = start_blocks(own_w, pos, rows, w.at[s], None, sem_a)
-        copies += start_blocks(oth_w, pos, rows, w.at[1 - s], None, sem_b)
+        copies = start_blocks(own_w, pos, 0, rows, w.at[s], None, sem_a)
+        copies += start_blocks(oth_w, pos, 0, rows, w.at[1 - s], None, sem_b)
         for copy in copies:
             copy.wait()
 
@@ -217,8 +277,8 @@
 
     @pl.when(pl.program_id(0) == 0)
     def _():
-        copies = start_blocks(left, pos, rows, wl, cols, sem_l)
-        copies += start_blocks(right, pos, rows, wr, None, sem_r)
+        copies = start_blocks(left, pos, 0, rows, wl, cols, sem_l)
+        copies += start_blocks(right, pos, 1, rows, wr, None, sem_r)
         for copy in copies:
             copy.wait()
         w[:, : wl.shape[1]] = wl[...]
@@ -271,8 +331,8 @@
 
     @pl.when(pl.program_id(0) == 0)
     def _():
-        copies = start_blocks(left, pos, rows, wl, None, sem_l)
-        copies += start_blocks(right, pos, rows, wr, None, sem_r)
+        copies = start_blocks(left, pos, 0, rows, wl, None, sem_l)
+        copies += start_blocks(right, pos, 1, rows, wr, None, sem_r)
         for copy in copies:
             copy.wait()
         w[:, : wl.shape[1]] = wl[...]
@@ -333,11 +393,12 @@
         send_ref[rel] = total[1 - s, at, :].astype(BF)
 
 
-def attend_back_kernel(meta, q_ref, k_ref, v_ref, e_ref, inv_ref, own_ref, oth_ref, dq_ref, dk_ref, dv_ref, off_ref, diag, dctx):
+def attend_back_kernel(meta, q_ref, k_ref, v_ref, e_ref, inv_ref, own_ref, oth_ref, dq_ref, dk_ref, dv_ref, off_ref, diag, dctx, table, low):
     s = meta[0]
     length = q_ref.shape[1]
     half = length // 2
     step = LANES
+    rows = step // 4
     n = pl.program_id(1)
     dctx[pl.ds(pl.multiple_of(s * half, half), half), :] = own_ref[0]
     dctx[pl.ds(pl.multiple_of((1 - s) * half, half), half), :] = oth_ref[0]
@@ -350,30 +411,27 @@
     scaled = (dctx[...].astype(F32) * inv).astype(BF)
     zero = jnp.zeros((), BF)
     first = lane_half((length, LANES), 0)
-    dq_parts = [None] * (length // step)
-    dk = jnp.zeros((length, LANES), F32)
-    dv = jnp.zeros((length, LANES), F32)
     for hh in range(2):
-        keep = first if hh == 0 else ~first
-        q_head, k_head, c_head = (jnp.where(keep, x, zero) for x in (q, k, scaled))
+        table[hh] = nt(jnp.where(first if hh == 0 else ~first, scaled, zero), v)
+    q_t, c_t = q.astype(F32).T.astype(BF), scaled.astype(F32).T.astype(BF)
+    dq, dk, dv = [], [], []
+    for hh in range(2):
         lane = hh * HEAD_DIM
-        for a in range(length // step):
-            at = slice(a * step, (a + 1) * step)
-            base = length - step - a * step
-            low = e_ref[0, 0, hh, at, :]
-            e = low.astype(F32)
-            term = e * nt(c_head[at], v)
-            delta = jnp.sum(term, axis=-1, keepdims=True) * inv[at, lane : lane + 1]
+        for at in range(0, length, rows):
+            base, within = length - step - at // step * step, at % step
+            e = e_ref[0, 0, hh, at : at + rows, :].astype(F32)
+            term = e * table[hh, at : at + rows]
+            delta = jnp.sum(term, axis=-1, keepdims=True) * inv[at : at + rows, lane : lane + 1]
             grad = term - e * delta
-            diag[hh, :, base : base + length] += grad
-            grad_low = grad.astype(BF)
-            part = nn(grad_low, k_head)
-            dq_parts[a] = part if hh == 0 else dq_parts[a] + part
-            dk = dk + tn(grad_low, q_head[at])
-            dv = dv + tn(low, c_head[at])
-    dq_ref[0] = jnp.concatenate(dq_parts, axis=0).astype(BF)
-    dk_ref[0] = dk.astype(BF)
-    dv_ref[0] = dv.astype(BF)
+            diag[hh, within : within + rows, base : base + length] += grad
+            low[hh, at : at + rows] = grad.astype(BF)
+        grad_low = low[hh]
+        dq.append(nn(grad_low, jnp.where(first if hh == 0 else ~first, k, zero)))
+        dk.append(nn(q_t[lane : lane + HEAD_DIM], grad_low))
+        dv.append(nn(c_t[lane : lane + HEAD_DIM], e_ref[0, 0, hh]))
+    dq_ref[0] = (dq[0] + dq[1]).astype(BF)
+    dk_ref[0] = jnp.concatenate(dk, axis=0).T.astype(BF)
+    dv_ref[0] = jnp.concatenate(dv, axis=0).T.astype(BF)
 
     @pl.when(n == pl.num_programs(1) - 1)
     def _():
@@ -471,47 +529,71 @@
     def sds(shape, dtype=BF):
         return jax.ShapeDtypeStruct(shape, dtype)
 
-    def columns(h):
+    def far(shape, dtype=BF):
+        return pltpu.HBM(shape, dtype)
+
+    def first_columns(h):
         cut = [lax.dynamic_slice_in_dim(w, h * half, half, 1) for w in (w_query, w_key, w_value)]
         table = jnp.pad(bias_table, (0, shard - table_rows))
         extra = jnp.stack([gain_attn, gain_ffn, table], axis=1)
         extra = jnp.pad(extra, ((0, 0), (0, LANES - 3)))
+        return jnp.concatenate(cut + [extra], axis=1)
+
+    def second_columns(h):
         out_cols = lax.dynamic_slice_in_dim(w_output, h * half, half, 1)
         in_cols = lax.dynamic_index_in_dim(ffn_in.reshape(shard, dp, 2, hid_rows), h, 2, keepdims=False)
-        return jnp.concatenate(cut + [extra, out_cols, in_cols.reshape(shard, hid)], axis=1)
-
-    mine, theirs = columns(s), other_core(columns(1 - s))
-    joined = jnp.where(s == 0, jnp.concatenate([mine, theirs]), jnp.concatenate([theirs, mine]))
+        return jnp.concatenate([out_cols, in_cols.reshape(shard, hid)], axis=1)
+
+    def swapped(mine, theirs):
+        theirs = other_core(theirs)
+        return jnp.where(s == 0, jnp.concatenate([mine, theirs]), jnp.concatenate([theirs, mine]))
+
+    first_cols = 3 * half + LANES
+    second_cols = half + hid
+    first_cut = (first_cols // LANES // 2) * LANES
+    second_cut = (second_cols // LANES // 2) * LANES
+    third_cut = (width // LANES // 2) * LANES
+
+    first = Gather(swapped(first_columns(s), first_columns(1 - s)), first_cut, dp)
+    first.high()
     x_oth = other_core(layer_input)
+    second_block = swapped(second_columns(s), second_columns(1 - s))
+    x_oth, second_block = meet((x_oth, second_block), (first, "have"))
+    second = Gather(second_block, second_cut, dp)
+    first.first()
+    second.high()
+    meet((), (first, "left right left_x right_y"))
+    first.second()
     g_oth = other_core(out_grad)
     keep_oth = other_core(keep_mask.astype(BF))
     keep = keep_mask.astype(BF)
     keep = jnp.where(s == 0, jnp.concatenate([keep, keep_oth], 1), jnp.concatenate([keep_oth, keep], 1))
     mask = ((keep.astype(F32) - 1.0) * 1e9)[:, None, :]
-    first_cols = 3 * half + LANES
-    first_cut = (first_cols // LANES // 2) * LANES
-    second_cut = ((half + hid) // LANES // 2) * LANES
-    third_cut = (width // LANES // 2) * LANES
-
-    first_l, first_r = gather_pieces(joined[:, :first_cols], first_cut, dp)
-    second_l, second_r = gather_pieces(joined[:, first_cols:], second_cut, dp)
-    third_l, third_r = gather_pieces(ffn_out, third_cut, dp)
+    x_oth, ffn_out = meet((x_oth, ffn_out), (first, "left right left_far right_far"), (second, "have"))
+    second.first()
+    third = Gather(ffn_out, third_cut, dp)
+    third.high()
 
     high = dp // 4
-    relative = np.array([(h << 2) | low for low in range(4) for h in range(high)], np.int32)
-    pos = (d ^ jnp.asarray(relative)).astype(jnp.int32)
-
-    def settle(pieces, cols=None):
+    orders = [np.array([(h << 2) | low for low in lows for h in range(high)], np.int32) for lows in ((0, 1, 2, 3), (0, 2, 1, 3))]
+    pos_l, pos_r = ((d ^ jnp.asarray(order)).astype(jnp.int32) for order in orders)
+    pos = pos_l
+
+    def settle(pieces, places=pos_l):
         if aligned:
             return pieces
         every = jnp.concatenate(pieces, axis=0)
-        order = jnp.argsort(pos)
+        order = jnp.argsort(places)
         return [every[order].reshape(1, -1, every.shape[-1])]
 
+    def settle_both(gather):
+        left, right = gather.pieces()
+        return settle(left), settle(right, pos_r)
+
     if not aligned:
-        pos_k, rows_k, hid_rows_k, nblk, dp_k = jnp.zeros((1,), jnp.int32), width, hid, 1, 1
+        pos_k, rows_k, hid_rows_k, nblk, dp_k = jnp.zeros((2, 1), jnp.int32), width, hid, 1, 1
     else:
-        pos_k, rows_k, hid_rows_k, nblk, dp_k = pos, rows, hid_rows, dp, dp
+        pos_k, rows_k, hid_rows_k, nblk, dp_k = jnp.stack([pos_l, pos_r]), rows, hid_rows, dp, dp
 
     feature = np.arange(width)
     chunk, within = feature // rows, feature % rows
@@ -528,7 +610,8 @@
     hsel, bsel = jnp.asarray(hsel), jnp.asarray(bsel)
     padded = jnp.concatenate([buckets, jnp.full((span - buckets.shape[0],), -1, jnp.int32)])[None]
 
-    a_l, a_r = settle(first_l), settle(first_r)
+    a_l, a_r = settle_both(first)
+
     seq_block = lambda shape: pl.BlockSpec((1,) + shape, lambda n: (n, 0, 0))
     q, k, v, normed_attn, misc, peroff, w_qkv = pl.pallas_call(
         functools.partial(
@@ -540,7 +623,7 @@
         out_specs=[seq_block((length, half))] * 3
         + [seq_block((length, width)), whole((8, width)), whole((8, span)), whole((width, first_cols))],
         out_shape=[sds((nseq, length, half))] * 3
-        + [sds((nseq, length, width)), sds((8, width), F32), sds((8, span), F32), sds((width, first_cols))],
+        + [far((nseq, length, width)), sds((8, width), F32), sds((8, span), F32), far((width, first_cols))],
         scratch_shapes=[
             pltpu.SemaphoreType.DMA((nblk,)),
             pltpu.SemaphoreType.DMA((nblk,)),
@@ -549,8 +632,11 @@
         ],
         compiler_params=params(),
         name="qkv",
+        cost_estimate=cost("qkv"),
     )(meta, pos_k, layer_input, x_oth, padded, hsel, bsel_once, *a_l, *a_r)
 
+    q, k, v = meet((q, k, v), (second, "left right left_x right_y"))
+    second.second()
     pair = pl.BlockSpec((1, length, LANES), lambda h, n: (n, 0, h))
     pair_half = pl.BlockSpec((1, count, LANES), lambda h, n: (n, 0, h))
     e_block = pl.BlockSpec((1, 1, 2, length, length), lambda h, n: (n, h, 0, 0, 0))
@@ -562,16 +648,23 @@
         out_shape=[
             sds((nseq, count, half)),
             sds((nseq, count, half)),
-            sds((nseq, pairs, 2, length, length)),
-            sds((nseq, length, half), F32),
+            far((nseq, pairs, 2, length, length)),
+            far((nseq, length, half), F32),
         ],
-        scratch_shapes=[pltpu.VMEM((2, LANES, span), F32), pltpu.VMEM((length, LANES), BF)],
+        scratch_shapes=[
+            pltpu.VMEM((2, LANES, span), F32),
+            pltpu.VMEM((length, LANES), BF),
+            pltpu.VMEM((2, length, length), F32),
+        ],
         compiler_params=params(),
         name="attend",
+        cost_estimate=cost("attend"),
     )(meta, q, k, v, mask, peroff)
+    ctx_own, ctx_send = meet((ctx_own, ctx_send), (second, "left right left_far right_far"), (third, "have"))
+    third.first()
     ctx_oth = other_core(ctx_send)
 
-    wo_own = jnp.concatenate([x[..., :half] for x in second_l], axis=0)
+    wo_own = jnp.concatenate([x[..., :half] for x in second.pieces()[0]], axis=0)
     wo_oth = other_core(wo_own)
     wo_own, wo_oth = settle([wo_own]), settle([wo_oth])
     middle, normed_ffn, w_o = pl.pallas_call(
@@ -579,14 +672,17 @@
         grid=(nseq,),
         in_specs=[SMEM, SMEM, seq_block((count, width)), seq_block((count, half)), seq_block((count, half)), whole((8, width)), ANY, ANY],
         out_specs=[seq_block((count, width)), seq_block((count, width)), whole((2, width, half))],
-        out_shape=[sds((nseq, count, width), F32), sds((nseq, count, width)), sds((2, width, half))],
+        out_shape=[far((nseq, count, width), F32), sds((nseq, count, width)), far((2, width, half))],
         scratch_shapes=[pltpu.SemaphoreType.DMA((nblk,)), pltpu.SemaphoreType.DMA((nblk,))],
         compiler_params=params(),
         name="middle",
+        cost_estimate=cost("middle"),
     )(meta, pos_k, layer_input, ctx_own, ctx_oth, misc, *wo_own, *wo_oth)
+    middle, normed_ffn = meet((middle, normed_ffn), (third, "left right left_x right_y"))
+    third.second()
     normed_oth = other_core(normed_ffn)
 
-    b_l, b_r = settle(second_l), settle(second_r)
+    b_l, b_r = settle_both(second)
     act, slope, w_in = pl.pallas_call(
         functools.partial(
             hidden_kernel, rows=rows_k, cols=(half, second_cut - half), nl=len(b_l), nr=len(b_r)
@@ -603,6 +699,7 @@
         ],
         compiler_params=params(),
         name="hidden",
+        cost_estimate=cost("hidden"),
     )(pos_k, normed_ffn, normed_oth, *b_l, *b_r)
 
     def block_outs(block_rows, cut, cols):
@@ -646,6 +743,7 @@
                 scratch_shapes=[pltpu.VMEM((m, cols), F32)] if aligned else [],
                 compiler_params=params(),
                 name=name,
+                cost_estimate=cost(name),
             )(meta, *a_list, *b_list),
             block_rows,
             cut,
@@ -653,16 +751,18 @@
 
     act_own, act_oth = act[:, :count], act[:, count:]
     grad_out_parts = wgrad([act_own, act_oth], [out_grad, g_oth], hid_rows, third_cut, "grad_ffn_out")
-    grad_ffn_out = scatter_pieces(*grad_out_parts, dp).astype(F32)
-
-    c_l, c_r = settle(third_l), settle(third_r)
+    grad_out_parts, slope, act = meet((grad_out_parts, slope, act), (third, "left right left_far right_far"))
+    out_sum = Scatter(grad_out_parts, dp)
+    out_sum.first()
+
+    c_l, c_r = settle_both(third)
     grad_pre, back_own, back_send, w_out = pl.pallas_call(
         functools.partial(ffn_back_kernel, rows=hid_rows_k, nl=len(c_l), nr=len(c_r)),
         grid=(nseq,),
         in_specs=[SMEM, seq_block((count, width)), seq_block((count, width)), seq_block((length, hid)), whole((width, hid))]
         + [ANY] * (len(c_l) + len(c_r)),
         out_specs=[seq_block((length, hid)), seq_block((count, width)), seq_block((count, width)), whole((hid, width))],
-        out_shape=[sds((nseq, length, hid)), sds((nseq, count, width), F32), sds((nseq, count, width)), sds((hid, width))],
+        out_shape=[sds((nseq, length, hid)), sds((nseq, count, width), F32), sds((nseq, count, width)), far((hid, width))],
         scratch_shapes=[
             pltpu.SemaphoreType.DMA((nblk,)),
             pltpu.SemaphoreType.DMA((nblk,)),
@@ -671,24 +771,18 @@
         ],
         compiler_params=params(),
         name="ffn_back",
+        cost_estimate=cost("ffn_back"),
     )(pos_k, out_grad, g_oth, slope, w_in, *c_l, *c_r)
+    grad_pre, back_own, back_send = meet((grad_pre, back_own, back_send), (out_sum, "left_got right_got"))
+    out_sum.second()
     back_oth = other_core(back_send)
 
     pre_own, pre_oth = grad_pre[:, :count], grad_pre[:, count:]
     in_cut = (hid // LANES // 2) * LANES
     grad_in_parts = wgrad([normed_ffn, normed_oth], [pre_own, pre_oth], rows, in_cut, "grad_ffn_in")
-    grad_in_block = scatter_pieces(*grad_in_parts, dp)
-
-    out_own, out_send = pl.pallas_call(
-        ffn_out_kernel,
-        grid=(nseq,),
-        in_specs=[seq_block((length, hid)), whole((hid, width))],
-        out_specs=[seq_block((count, width)), seq_block((count, width))],
-        out_shape=[sds((nseq, count, width), F32), sds((nseq, count, width))],
-        compiler_params=params(),
-        name="ffn_out",
-    )(act, w_out)
-    layer_out = (middle + out_own + other_core(out_send).astype(F32)).astype(BF)
+    grad_in_parts, back_own, back_oth = meet((grad_in_parts, back_own, back_oth), (out_sum, "left_got right_got"))
+    out_sum.join()
+    out_sum.send()
 
     grad_middle, middle_low, dctx_own, dctx_send = pl.pallas_call(
         middle_back_kernel,
@@ -703,6 +797,7 @@
         ],
         compiler_params=params(),
         name="middle_back",
+        cost_estimate=cost("middle_back"),
     )(meta, out_grad, middle, back_own, back_oth, misc, w_o)
     dctx_oth = other_core(dctx_send)
 
@@ -716,6 +811,7 @@
         grid=(1,),
         compiler_params=params(),
         name="grad_output",
+        cost_estimate=cost("grad_output"),
     )(rel_meta, ctx_own, ctx_oth, middle_low)
     wo_sum = (wo_keep.astype(F32) + other_core(wo_send).astype(F32)).astype(BF)
     if not aligned:
@@ -725,7 +821,9 @@
     wo_left = jnp.swapaxes(by_bits[..., :wo_cut], 0, 2)
     wo_right = jnp.moveaxis(by_bits[..., wo_cut:], 0, 2)
     wo_parts = (wo_left[:, 1], wo_left[:, 0], wo_right[:, 1], wo_right[:, 0])
-    wo_block = scatter_pieces(*wo_parts, dp)
+    wo_parts, dctx_own, dctx_oth, act = meet((wo_parts, dctx_own, dctx_oth, act))
+    in_sum = Scatter([jnp.concatenate(pair, axis=-1) for pair in zip(grad_in_parts, wo_parts)], dp)
+    in_sum.first()
 
     dq, dk, dv, off = pl.pallas_call(
         attend_back_kernel,
@@ -733,11 +831,23 @@
         in_specs=[SMEM, pair, pair, pair, e_block, pair, pair_half, pair_half],
         out_specs=[pair, pair, pair, pl.BlockSpec((1, 2, span), lambda h, n: (h, 0, 0))],
         out_shape=[sds((nseq, length, half))] * 3 + [sds((pairs, 2, span), F32)],
-        scratch_shapes=[pltpu.VMEM((2, LANES, span), F32), pltpu.VMEM((length, LANES), BF)],
+        scratch_shapes=[
+            pltpu.VMEM((2, LANES, span), F32),
+            pltpu.VMEM((length, LANES), BF),
+            pltpu.VMEM((2, length, length), F32),
+            pltpu.VMEM((2, length, length), BF),
+        ],
         compiler_params=params(),
         name="attend_back",
+        cost_estimate=cost("attend_back"),
     )(meta, q, k, v, expo, inv, dctx_own, dctx_oth)
+    dq, dk, dv, off = meet(
+        (dq, dk, dv, off), (out_sum, "got"), (in_sum, "left_got right_got")
+    )
+    out_sum.take()
+    in_sum.second()
     off = jnp.pad(off.reshape(half_heads, span), ((0, 8 - half_heads), (0, 0)))
+    out_block = out_sum.rest()
 
     mb = 384
     shapes = block_outs(rows, first_cut, first_cols)
@@ -760,11 +870,28 @@
             scratch_shapes=[pltpu.VMEM((width, first_cols), F32)],
             compiler_params=params(),
             name="grad_qkv",
+        cost_estimate=cost("grad_qkv"),
         )(meta, normed_attn, dq, dk, dv, off, padded, hsel, bsel),
         rows,
         first_cut,
     )
-    qkv_block = scatter_pieces(*qkv_parts, dp)
+    qkv_parts, dq, dk, dv = meet((qkv_parts, dq, dk, dv), (in_sum, "left_got right_got"))
+    qkv_sum = Scatter(qkv_parts, dp)
+    qkv_sum.first()
+    in_sum.join()
+    in_sum.send()
+
+    out_own, out_send = pl.pallas_call(
+        ffn_out_kernel,
+        grid=(nseq,),
+        in_specs=[seq_block((length, hid)), whole((hid, width))],
+        out_specs=[seq_block((count, width)), seq_block((count, width))],
+        out_shape=[sds((nseq, count, width), F32), sds((nseq, count, width))],
+        compiler_params=params(),
+        name="ffn_out",
+        cost_estimate=cost("ffn_out"),
+    )(act, w_out)
+    layer_out = (middle + out_own + other_core(out_send).astype(F32)).astype(BF)
 
     dn_own, dn_send = pl.pallas_call(
         input_grad_kernel,
@@ -774,7 +901,10 @@
         out_shape=[sds((nseq, count, width), F32), sds((nseq, count, width))],
         compiler_params=params(),
         name="input_grad",
+        cost_estimate=cost("input_grad"),
     )(meta, dq, dk, dv, w_qkv)
+    dn_own, dn_oth, layer_out = meet((dn_own, other_core(dn_send), layer_out), (qkv_sum, "left_got right_got"))
+    qkv_sum.second()
     grad_input = pl.pallas_call(
         last_kernel,
         grid=(nseq,),
@@ -783,7 +913,14 @@
         out_shape=sds((nseq, count, width)),
         compiler_params=params(),
         name="last",
-    )(layer_input, grad_middle, dn_own, other_core(dn_send), misc)
+        cost_estimate=cost("last"),
+    )(layer_input, grad_middle, dn_own, dn_oth, misc)
+
+    grad_input = meet(grad_input, (qkv_sum, "left_got right_got"), (in_sum, "got"))
+    qkv_sum.join()
+    in_sum.take()
+    qkv_block, in_wo_block = qkv_sum.rest(), in_sum.rest()
+    grad_ffn_out = out_block.astype(F32)
 
     def both_cores(block):
         mine = lax.dynamic_slice_in_dim(block, s * shard, shard, 0)
@@ -791,11 +928,16 @@
         first, last = jnp.where(s == 0, mine, theirs), jnp.where(s == 0, theirs, mine)
         return first.astype(F32), last.astype(F32)
 
-    in_first, in_last = both_cores(grad_in_block)
+    in_first, in_last = both_cores(in_wo_block)
+    wo_first, wo_last = (
+        jnp.concatenate([x[:, in_cut : in_cut + wo_cut], x[:, wo_cut + hid :]], axis=1) for x in (in_first, in_last)
+    )
+    in_first, in_last = (
+        jnp.concatenate([x[:, :in_cut], x[:, in_cut + wo_cut : wo_cut + hid]], axis=1) for x in (in_first, in_last)
+    )
     grad_ffn_in = jnp.stack(
         [in_first.reshape(shard, dp, hid_rows), in_last.reshape(shard, dp, hid_rows)], axis=2
     ).reshape(shard, 2 * hid)
-    wo_first, wo_last = both_cores(wo_block)
     grad_output = jnp.concatenate([wo_first, wo_last], axis=1)
     qkv_first, qkv_last = both_cores(qkv_block)
     grad_query, grad_key, grad_value = (

time: 411 us -> 263 us (0.64)
  waiting for transfers between devices: 147 us -> 56.9 us
  Pallas kernels: 161 us -> 114 us
  local copies, waits for them, and re-layouts: 24.2 us -> 18.3 us
    ppermute x48 -> x42, waiting for transfers between devices: 145 us -> 55.9 us  [flip(): return lax.ppermute(x, axis, [(i, i ^ bit) for i in range(count)])]
    pallas_call x1, Pallas kernels: 34.6 us -> 20.9 us  [body(): pl.pallas_call(attend_back_kernel, grid=(pairs, nseq), in_specs=[SMEM, pa...]
    pallas_call x1, Pallas kernels: 24.7 us -> 14.2 us  [body(): pl.pallas_call(attend_kernel, grid=(pairs, nseq), in_specs=[SMEM, pair, p...]
    pallas_call x2, Pallas kernels: 17.1 us -> 12.2 us  [wgrad(): pl.pallas_call(functools.partial(kernel, na=len(a_list), nb=len(b_list),...]
    slice x1, local copies, waits for them, and re-layouts: 5.05 us -> 0.55 us  [body(): act_own, act_oth = (act[:, :count], act[:, count:])]
    ppermute x48 -> x42, starting transfers between devices: 55.4 us -> 53.3 us  [flip(): return lax.ppermute(x, axis, [(i, i ^ bit) for i in range(count)])]
  transfers between devices with their start and end apart: 63 -> 57, of which waited for: 31 -> 18; matrix products, arithmetic and copies ran while one was open for 8% -> 8% of each run, Pallas kernels for 31% -> 41%
where the time goes in v2:
time: 263 us; the launch traced here: 262 us
  Pallas kernels  114 us (43%)
  waiting for transfers between devices  56.9 us (22%)
  starting transfers between devices  55.8 us (21%)
  local copies, waits for them, and re-layouts  18.3 us (7%)
  other arithmetic  15.3 us (6%)
    ppermute x42, waiting for transfers between devices, flip(): return lax.ppermute(x, axis, [(i, i ^ bit) for i in range(count)])  55.9 us
    ppermute x42, starting transfers between devices, flip(): return lax.ppermute(x, axis, [(i, i ^ bit) for i in range(count)])  53.3 us
    pallas_call x1, Pallas kernels, body(): pl.pallas_call(attend_back_kernel, grid=(pairs, nseq), in_specs=[SMEM, pa...  20.9 us
    pallas_call x1, Pallas kernels, body(): pl.pallas_call(attend_kernel, grid=(pairs, nseq), in_specs=[SMEM, pair, p...  14.2 us
    pallas_call x1, Pallas kernels, body(): pl.pallas_call(functools.partial(ffn_back_kernel, rows=hid_rows_k, nl=len...  13.8 us
    pallas_call x2, Pallas kernels, wgrad(): pl.pallas_call(functools.partial(kernel, na=len(a_list), nb=len(b_list),...  12.2 us
    pallas_call x1, Pallas kernels, body(): pl.pallas_call(functools.partial(hidden_kernel, rows=rows_k, cols=(half,...  12 us
    pallas_call x1, Pallas kernels, body(): pl.pallas_call(functools.partial(qkv_kernel, rows=rows_k, cut=first_cut,...  10.1 us
  transfers between devices with their start and end apart: 57, of which 18 were waited for; matrix products, arithmetic and copies ran while one was open for 8% of the time, Pallas kernels for 41%

profile of v2, /device:TPU:0, one launch (start us, length us, event | category | flops | bytes accessed | tf_op | source)
XLA Modules:
  0.0 262.0 jit_solution(14264404915813491928)
XLA Ops:
  7.8 5.1 %collective-permute-start.5 = (bf16[1,48,1280]{2,1,0:T(8,128)(2,1)S(1)}, bf16[1,48,1280]{2,1,0:T(8,128)(2,1)S(1)}, u32[]{:S(2)}, u32[]{:S(2)}) collective-permute-start(bf16[1,48,1280]{2,1,0:T(8,128)(2,1)S(1)} %maximum_select_fusion.1), channel_id=1, source_target_pairs={{0,24},{2,26},{4,28},{6,30},{8,16},{10,18},{12,20},{14,22},{16,8},... | collective-permute-start | bytes 368648 | tf_op jit(solution)/shard_map/ppermute | solution.py:58
  13.6 3.5 %collective-permute-done.5 = bf16[1,48,1280]{2,1,0:T(8,128)(2,1)S(1)} collective-permute-done((bf16[1,48,1280]{2,1,0:T(8,128)(2,1)S(1)}, bf16[1,48,1280]{2,1,0:T(8,128)(2,1)S(1)}, u32[]{:S(2)}, u32[]{:S(2)}) %collective-permute-start.5) | collective-permute-done | bytes 122912 | tf_op jit(solution)/shard_map/ppermute | solution.py:58
  17.1 6.4 %collective-permute-done.4 = bf16[1,48,1280]{2,1,0:T(8,128)(2,1)S(1)} collective-permute-done((bf16[1,48,1280]{2,1,0:T(8,128)(2,1)S(1)}, bf16[1,48,1280]{2,1,0:T(8,128)(2,1)S(1)}, u32[]{:S(2)}, u32[]{:S(2)}) %collective-permute-start.4) | collective-permute-done | bytes 122912 | tf_op jit(solution)/shard_map/ppermute | solution.py:58
  26.8 4.0 %collective-permute-done.7 = bf16[4,48,640]{2,1,0:T(8,128)(2,1)S(1)} collective-permute-done((bf16[4,48,640]{2,1,0:T(8,128)(2,1)S(1)}, bf16[4,48,640]{2,1,0:T(8,128)(2,1)S(1)}, u32[]{:S(2)}, u32[]{:S(2)}) %collective-permute-start.7) | collective-permute-done | bytes 245792 | tf_op jit(solution)/shard_map/ppermute | solution.py:58
  38.9 4.8 %collective-permute-done.12 = bf16[1,48,1920]{2,1,0:T(8,128)(2,1)S(1)} collective-permute-done((bf16[1,48,1920]{2,1,0:T(8,128)(2,1)S(1)}, bf16[1,48,1920]{2,1,0:T(8,128)(2,1)S(1)}, u32[]{:S(2)}, u32[]{:S(2)}) %collective-permute-start.12) | collective-permute-done | bytes 184352 | tf_op jit(solution)/shard_map/ppermute | solution.py:58
  43.8 6.4 %collective-permute-done.11 = bf16[1,48,1920]{2,1,0:T(8,128)(2,1)S(1)} collective-permute-done((bf16[1,48,1920]{2,1,0:T(8,128)(2,1)S(1)}, bf16[1,48,1920]{2,1,0:T(8,128)(2,1)S(1)}, u32[]{:S(2)}, u32[]{:S(2)}) %collective-permute-start.11) | collective-permute-done | bytes 184352 | tf_op jit(solution)/shard_map/ppermute | solution.py:58
  50.3 2.8 %collective-permute-start.20 = (bf16[1,96,768]{2,1,0:T(8,128)(2,1)S(1)}, bf16[1,96,768]{2,1,0:T(8,128)(2,1)S(1)}, u32[]{:S(2)}, u32[]{:S(2)}) collective-permute-start(bf16[1,96,768]{2,1,0:T(8,128)(2,1)S(1)} %bitcast.110), channel_id=1, source_target_pairs={{0,24},{2,26},{4,28},{6,30},{8,16},{10,18},{12,20},{14,22},{16,8},... | collective-permute-start | bytes 442376 | tf_op jit(solution)/shard_map/ppermute | solution.py:58
  56.9 10.1 %qkv.1 = (bf16[3,512,384]{2,1,0:T(8,128)(2,1)S(1)}, bf16[3,512,384]{2,1,0:T(8,128)(2,1)S(1)}, bf16[3,512,384]{2,1,0:T(8,128)(2,1)S(1)}, bf16[3,512,768]{2,1,0:T(...) custom-call(s32[2]{0:T(128)S(1)} %pad_add_fusion.2.meta, ...), custom_call_target="tpu_custom_call" | custom-call | flops 11500000256 | tf_op jit(solution)/shard_map/qkv/pallas_call | solution.py:616
  69.5 14.2 %attend.1 = (bf16[3,256,384]{2,1,0:T(8,128)(2,1)S(1)}, bf16[3,256,384]{2,1,0:T(8,128)(2,1)S(1)}, bf16[3,3,2,512,512]{4,3,2,1,0:T(8,128)(2,1)}, f32[3,512,384]{2,1,0:T(8,128)}) custom-call(s32[2]{0:T(128)S(1)} %pad_add_fusion.2.meta, bf16[3,512,384]{2,1,0:T(8,128)(2,1)S(1)} %get-tuple-element.168.q_ref, bf16[3,512,384]{2,1,0:T(8,128)(2,1)S(1)} %get-tuple-element.169.k_ref, ...), custom_call_target="tpu_custom_call" | custom-call | flops 28750000128 | tf_op jit(solution)/shard_map/attend/pallas_call | solution.py:643
  87.9 6.4 %middle.1 = (f32[3,256,768]{2,1,0:T(8,128)}, bf16[3,256,768]{2,1,0:T(8,128)(2,1)}, bf16[2,768,384]{2,1,0:T(8,128)(2,1)}) custom-call(s32[2]{0:T(128)S(1)} %pad_add_fusion.2.meta, s32[2,16]{1,0:T(2,128)S(1)} %pad_add_fusion.1.pos, bf16[3,256,768]{2,1,0:T(8,128)(2,1)S(1)} %copy-done.8, bf16[3,256,384]{2,1,0:T(8,128)(2,1)S(1)} %get-tuple-element.181.own_ref, ...), custom_call_target="tpu_custom_call" | custom-call | flops 8049999872 | tf_op jit(solution)/shard_map/middle/pallas_call | solution.py:670
  100.7 12.0 %hidden.1 = (bf16[3,512,1536]{2,1,0:T(8,128)(2,1)S(1)}, bf16[3,512,1536]{2,1,0:T(8,128)(2,1)S(1)}, bf16[768,1536]{1,0:T(8,128)(2,1)S(1)}) custom-call(s32[2,16]{1,0:T(2,128)S(1)} %pad_add_fusion.1.pos, bf16[3,256,768]{2,1,0:T(8,128)(2,1)} %get-tuple-element.190.own_ref.rest_0_, bf16[3,256,768]{2,1,0:T(8,128)(2,1)} %collective-permute-done.25.oth_ref.rest_1_, ...), custom_call_target="tpu_custom_call" | custom-call | flops 13799999488 | tf_op jit(solution)/shard_map/hidden/pallas_call | solution.py:686
  113.3 6.5 %grad_ffn_out.1 = (bf16[2,4,96,384]{3,2,1,0:T(8,128)(2,1)S(1)}, bf16[2,4,96,384]{3,2,1,0:T(8,128)(2,1)S(1)}, bf16[2,4,96,384]{3,2,1,0:T(8,128)(2,1)S(1)}, bf16[2,4,96,384]{3,2,1,0:T(8,128)(2,1)S(1)}) custom-call(s32[2]{0:T(128)S(1)} %pad_add_fusion.2.meta, bf16[3,256,1536]{2,1,0:T(8,128)(2,1)S(1)} %get-tuple-element.302.rest_0_, ...), custom_call_target="tpu_custom_call" | custom-call | flops 10350000128 | tf_op jit(solution)/shard_map/grad_ffn_out/pallas_call | solution.py:735
  121.9 13.8 %ffn_back.1 = (bf16[3,512,1536]{2,1,0:T(8,128)(2,1)S(1)}, f32[3,256,768]{2,1,0:T(8,128)S(1)}, bf16[3,256,768]{2,1,0:T(8,128)(2,1)S(1)}, bf16[1536,768]{1,0:T(8,128)(2,1)}) custom-call(s32[2,16]{1,0:T(2,128)S(1)} %pad_add_fusion.1.pos, bf16[3,256,768]{2,1,0:T(8,128)(2,1)S(1)} %copy-done.6, bf16[3,256,768]{2,1,0:T(8,128)(2,1)} %collective-permute-done.26.rest_3_.g_oth, ...), custom_call_target="tpu_custom_call" | custom-call | flops 17250000896 | tf_op jit(solution)/shard_map/ffn_back/pallas_call | solution.py:759
  138.9 5.7 %grad_ffn_in.1 = (bf16[2,4,48,768]{3,2,1,0:T(8,128)(2,1)S(1)}, bf16[2,4,48,768]{3,2,1,0:T(8,128)(2,1)S(1)}, bf16[2,4,48,768]{3,2,1,0:T(8,128)(2,1)S(1)}, bf16[2,4,48,768]{3,2,1,0:T(8,128)(2,1)S(1)}) custom-call(s32[2]{0:T(128)S(1)} %pad_add_fusion.2.meta, bf16[3,256,768]{2,1,0:T(8,128)(2,1)} %get-tuple-element.190.own_ref.rest_0_, ...), custom_call_target="tpu_custom_call" | custom-call | flops 10350000128 | tf_op jit(solution)/shard_map/grad_ffn_in/pallas_call | solution.py:735
  147.0 3.5 %middle_back.1 = (f32[3,256,768]{2,1,0:T(8,128)S(1)}, bf16[3,256,768]{2,1,0:T(8,128)(2,1)S(1)}, bf16[3,256,384]{2,1,0:T(8,128)(2,1)S(1)}, bf16[3,256,384]{2,1,0:T(8,128)(2,1)S(1)}) custom-call(s32[2]{0:T(128)S(1)} %pad_add_fusion.2.meta, bf16[3,256,768]{2,1,0:T(8,128)(2,1)S(1)} %copy-done.7, f32[3,256,768]{2,1,0:T(8,128)S(1)} %copy-done, ...), custom_call_target="tpu_custom_call" | custom-call | flops 8049999872 | tf_op jit(solution)/shard_map/middle_back/pallas_call | solution.py:787
  163.7 20.9 %attend_back.1 = (bf16[3,512,384]{2,1,0:T(8,128)(2,1)S(1)}, bf16[3,512,384]{2,1,0:T(8,128)(2,1)S(1)}, bf16[3,512,384]{2,1,0:T(8,128)(2,1)S(1)}, f32[3,2,1024]{2,1,0:T(2,128)S(1)}) custom-call(s32[2]{0:T(128)S(1)} %pad_add_fusion.2.meta, bf16[3,512,384]{2,1,0:T(8,128)(2,1)S(1)} %copy-done.34, bf16[3,512,384]{2,1,0:T(8,128)(2,1)S(1)} %copy-done.36, ...), custom_call_target="tpu_custom_call" | custom-call | flops 40249999360 | tf_op jit(solution)/shard_map/attend_back/pallas_call | solution.py:828
  184.7 4.9 %ffn_out.1 = (f32[3,256,768]{2,1,0:T(8,128)S(1)}, bf16[3,256,768]{2,1,0:T(8,128)(2,1)}) custom-call(bf16[3,512,1536]{2,1,0:T(8,128)(2,1)S(1)} %get-tuple-element.266.act_ref, bf16[1536,768]{1,0:T(8,128)(2,1)S(1)} %copy-done.20), custom_call_target="tpu_custom_call" | custom-call | flops 9200000000 | tf_op jit(solution)/shard_map/ffn_out/pallas_call | solution.py:884
  199.6 6.6 %grad_qkv.1 = (bf16[2,4,48,640]{3,2,1,0:T(8,128)(2,1)S(1)}, bf16[2,4,48,640]{3,2,1,0:T(8,128)(2,1)S(1)}, bf16[2,4,48,640]{3,2,1,0:T(8,128)(2,1)S(1)}, bf16[2,4,48,640]{3,2,1,0:T(8,128)(2,1)S(1)}) custom-call(s32[2]{0:T(128)S(1)} %pad_add_fusion.2.meta, bf16[3,512,768]{2,1,0:T(8,128)(2,1)S(1)} %copy-done.25, bf16[3,512,384]{2,1,0:T(8,128)(2,1)S(1)} %copy-done.27, ...), custom_call_target="tpu_custom_call" | custom-call | flops 11500000256 | tf_op jit(solution)/shard_map/grad_qkv/pallas_call | solution.py:862
  208.8 4.8 %input_grad.1 = (f32[3,256,768]{2,1,0:T(8,128)S(1)}, bf16[3,256,768]{2,1,0:T(8,128)(2,1)S(1)}) custom-call(s32[2]{0:T(128)S(1)} %pad_add_fusion.2.meta, bf16[3,512,384]{2,1,0:T(8,128)(2,1)S(1)} %copy-done.27, bf16[3,512,384]{2,1,0:T(8,128)(2,1)S(1)} %copy-done.29, bf16[3,512,384]{2,1,0:T(8,128)(2,1)S(1)} %copy-done.32, bf16[768,1280]{1,0:T(8,128)(2,1)S(1)} %copy-done.24), custom_call_target="tpu_custom_call" | custom-call | flops 9200000000 | tf_op jit(solution)/shard_map/input_grad/pallas_call | solution.py:896
  214.5 2.7 %add_convert_fusion = bf16[3,256,768]{2,1,0:T(8,128)(2,1)} fusion(bf16[3,256,768]{2,1,0:T(8,128)(2,1)} %collective-permute-done.44, f32[3,256,768]{2,1,0:T(8,128)S(1)} %copy-done, f32[3,256,768]{2,1,0:T(8,128)S(1)} %copy-done.2), kind=kLoop, calls=%fused_computation | loop fusion | flops 2359296 | bytes 7077888 | tf_op jit(solution)/shard_map/convert_element_type | solution.py:894
  221.9 8.9 %collective-permute-done.45 = bf16[2,4,48,640]{3,2,1,0:T(8,128)(2,1)S(1)} collective-permute-done((bf16[2,4,48,640]{3,2,1,0:T(8,128)(2,1)S(1)}, bf16[2,4,48,640]{3,2,1,0:T(8,128)(2,1)S(1)}, u32[]{:S(2)}, u32[]{:S(2)}) %collective-permute-start.45) | collective-permute-done | bytes 491552 | tf_op jit(solution)/shard_map/ppermute | solution.py:58
  236.5 5.4 %collective-permute-done.50 = bf16[1,48,1920]{2,1,0:T(8,128)(2,1)S(1)} collective-permute-done((bf16[1,48,1920]{2,1,0:T(8,128)(2,1)S(1)}, bf16[1,48,1920]{2,1,0:T(8,128)(2,1)S(1)}, u32[]{:S(2)}, u32[]{:S(2)}) %collective-permute-start.50) | collective-permute-done | bytes 184352 | tf_op jit(solution)/shard_map/ppermute | solution.py:58
  248.1 3.3 %collective-permute-done.54 = bf16[1,48,1280]{2,1,0:T(8,128)(2,1)S(1)} collective-permute-done((bf16[1,48,1280]{2,1,0:T(8,128)(2,1)S(1)}, bf16[1,48,1280]{2,1,0:T(8,128)(2,1)S(1)}, u32[]{:S(2)}, u32[]{:S(2)}) %collective-permute-start.54) | collective-permute-done | bytes 122912 | tf_op jit(solution)/shard_map/ppermute | solution.py:58
  251.3 5.8 %collective-permute-done.53 = bf16[1,48,1280]{2,1,0:T(8,128)(2,1)S(1)} collective-permute-done((bf16[1,48,1280]{2,1,0:T(8,128)(2,1)S(1)}, bf16[1,48,1280]{2,1,0:T(8,128)(2,1)S(1)}, u32[]{:S(2)}, u32[]{:S(2)}) %collective-permute-start.53) | collective-permute-done | bytes 122912 | tf_op jit(solution)/shard_map/ppermute | solution.py:58
  (366 shorter events, 91.2 us)
Async XLA Ops:
  1.4 35.5 %collective-permute-start.15 = (bf16[3,256]{1,0:T(4,128)(2,1)S(1)}, bf16[3,256]{1,0:T(4,128)(2,1)S(1)}, u32[]{:S(2)}, u32[]{:S(2)}) collective-permute-start(bf16[3,256]{1,0:T(4,128)(2,1)S(1)} %convert_element_type.247), channel_id=1, source_target_pairs={{0,1},{1,0},{2,3},{3,2},{4,5},{5,4},{6,7},{7,6},{8,9},{9,8},{10,11... | collective-permute-start | bytes 4616 | tf_op jit(solution)/shard_map/ppermute | solution.py:148
  4.3 19.2 %collective-permute-start = (bf16[3,256,768]{2,1,0:T(8,128)(2,1)}, bf16[3,256,768]{2,1,0:T(8,128)(2,1)S(1)}, u32[]{:S(2)}, u32[]{:S(2)}) collective-permute-start(bf16[3,256,768]{2,1,0:T(8,128)(2,1)} %x_ref.3), channel_id=1, source_target_pairs={{0,1},{1,0},{2,3},{3,2},{4,5},{5,4},{6,7},{7,6},{8,9},{9,8},{10,11... | collective-permute-start | bytes 3538952 | tf_op jit(solution)/shard_map/ppermute | solution.py:148
  32.1 18.1 %collective-permute-start.9 = (bf16[8,48,640]{2,1,0:T(8,128)(2,1)S(1)}, bf16[8,48,640]{2,1,0:T(8,128)(2,1)S(1)}, u32[]{:S(2)}, u32[]{:S(2)}) collective-permute-start(bf16[8,48,640]{2,1,0:T(8,128)(2,1)S(1)} %constant_dynamic-update-slice_fusion.2.rest_2_), channel_id=1, source_target_pairs={{0,2},{2,0},{4,6},{6,4},{8,10},{10,8},{12,14},{14,12},{16,18},{18,... | collective-permute-start | bytes 1474568 | tf_op jit(solution)/shard_map/ppermute | solution.py:58
  33.7 16.5 %collective-permute-start.8 = (bf16[8,48,640]{2,1,0:T(8,128)(2,1)S(1)}, bf16[8,48,640]{2,1,0:T(8,128)(2,1)S(1)}, u32[]{:S(2)}, u32[]{:S(2)}) collective-permute-start(bf16[8,48,640]{2,1,0:T(8,128)(2,1)S(1)} %constant_dynamic-update-slice_fusion.rest_0_), channel_id=1, source_target_pairs={{0,4},{2,6},{4,0},{6,2},{8,12},{10,14},{12,8},{14,10},{16,20},{18,... | collective-permute-start | bytes 1474568 | tf_op jit(solution)/shard_map/ppermute | solution.py:58
  50.3 16.8 %collective-permute-start.20 = (bf16[1,96,768]{2,1,0:T(8,128)(2,1)S(1)}, bf16[1,96,768]{2,1,0:T(8,128)(2,1)S(1)}, u32[]{:S(2)}, u32[]{:S(2)}) collective-permute-start(bf16[1,96,768]{2,1,0:T(8,128)(2,1)S(1)} %bitcast.110), channel_id=1, source_target_pairs={{0,24},{2,26},{4,28},{6,30},{8,16},{10,18},{12,20},{14,22},{16,8},... | collective-permute-start | bytes 442376 | tf_op jit(solution)/shard_map/ppermute | solution.py:58
  53.1 14.0 %collective-permute-start.19 = (bf16[1,96,768]{2,1,0:T(8,128)(2,1)S(1)}, bf16[1,96,768]{2,1,0:T(8,128)(2,1)S(1)}, u32[]{:S(2)}, u32[]{:S(2)}) collective-permute-start(bf16[1,96,768]{2,1,0:T(8,128)(2,1)S(1)} %bitcast.111), channel_id=1, source_target_pairs={{0,16},{2,18},{4,20},{6,22},{8,24},{10,26},{12,28},{14,30},{16,0},... | collective-permute-start | bytes 442376 | tf_op jit(solution)/shard_map/ppermute | solution.py:58
  53.1 14.0 %collective-permute-start.18 = (bf16[1,96,768]{2,1,0:T(8,128)(2,1)S(1)}, bf16[1,96,768]{2,1,0:T(8,128)(2,1)S(1)}, u32[]{:S(2)}, u32[]{:S(2)}) collective-permute-start(bf16[1,96,768]{2,1,0:T(8,128)(2,1)S(1)} %bitcast.112), channel_id=1, source_target_pairs={{0,8},{2,10},{4,12},{6,14},{8,0},{10,2},{12,4},{14,6},{16,24},{18,... | collective-permute-start | bytes 442376 | tf_op jit(solution)/shard_map/ppermute | solution.py:58
  67.3 16.4 %collective-permute-start.16 = (bf16[8,48,896]{2,1,0:T(8,128)(2,1)S(1)}, bf16[8,48,896]{2,1,0:T(8,128)(2,1)S(1)}, u32[]{:S(2)}, u32[]{:S(2)}) collective-permute-start(bf16[8,48,896]{2,1,0:T(8,128)(2,1)S(1)} %constant_dynamic-update-slice_fusion.4.rest_0_), channel_id=1, source_target_pairs={{0,4},{2,6},{4,0},{6,2},{8,12},{10,14},{12,8},{14,10},{16,20},{18,... | collective-permute-start | bytes 2064392 | tf_op jit(solution)/shard_map/ppermute | solution.py:58
  68.0 16.0 %collective-permute-start.17 = (bf16[8,48,1024]{2,1,0:T(8,128)(2,1)S(1)}, bf16[8,48,1024]{2,1,0:T(8,128)(2,1)S(1)}, u32[]{:S(2)}, u32[]{:S(2)}) collective-permute-start(bf16[8,48,1024]{2,1,0:T(8,128)(2,1)S(1)} %constant_dynamic-update-slice_fusion.6.rest_2_), channel_id=1, source_target_pairs={{0,2},{2,0},{4,6},{6,4},{8,10},{10,8},{12,14},{14,12},{16,18},{18,... | collective-permute-start | bytes 2359304 | tf_op jit(solution)/shard_map/ppermute | solution.py:58
  95.8 17.5 %collective-permute-start.26 = (bf16[3,256,768]{2,1,0:T(8,128)(2,1)S(1)}, bf16[3,256,768]{2,1,0:T(8,128)(2,1)}, u32[]{:S(2)}, u32[]{:S(2)}) collective-permute-start(bf16[3,256,768]{2,1,0:T(8,128)(2,1)S(1)} %copy-done.6), channel_id=1, source_target_pairs={{0,1},{1,0},{2,3},{3,2},{4,5},{5,4},{6,7},{7,6},{8,9},{9,8},{10,11... | collective-permute-start | bytes 3538952 | tf_op jit(solution)/shard_map/ppermute | solution.py:148
  98.4 21.4 %collective-permute-start.28 = (bf16[8,96,384]{2,1,0:T(8,128)(2,1)S(1)}, bf16[8,96,384]{2,1,0:T(8,128)(2,1)S(1)}, u32[]{:S(2)}, u32[]{:S(2)}) collective-permute-start(bf16[8,96,384]{2,1,0:T(8,128)(2,1)S(1)} %constant_dynamic-update-slice_fusion.10.rest_2_), channel_id=1, source_target_pairs={{0,2},{2,0},{4,6},{6,4},{8,10},{10,8},{12,14},{14,12},{16,18},{18,... | collective-permute-start | bytes 1769480 | tf_op jit(solution)/shard_map/ppermute | solution.py:58
  100.0 19.8 %collective-permute-start.27 = (bf16[8,96,384]{2,1,0:T(8,128)(2,1)S(1)}, bf16[8,96,384]{2,1,0:T(8,128)(2,1)S(1)}, u32[]{:S(2)}, u32[]{:S(2)}) collective-permute-start(bf16[8,96,384]{2,1,0:T(8,128)(2,1)S(1)} %constant_dynamic-update-slice_fusion.8.rest_0_), channel_id=1, source_target_pairs={{0,4},{2,6},{4,0},{6,2},{8,12},{10,14},{12,8},{14,10},{16,20},{18,... | collective-permute-start | bytes 1769480 | tf_op jit(solution)/shard_map/ppermute | solution.py:58
  119.8 15.9 %collective-permute-start.29 = (bf16[2,4,96,384]{3,2,1,0:T(8,128)(2,1)S(1)}, bf16[2,4,96,384]{3,2,1,0:T(8,128)(2,1)S(1)}, u32[]{:S(2)}, u32[]{:S(2)}) collective-permute-start(bf16[2,4,96,384]{3,2,1,0:T(8,128)(2,1)S(1)} %get-tuple-element.212), channel_id=1, source_target_pairs={{0,4},{2,6},{4,0},{6,2},{8,12},{10,14},{12,8},{14,10},{16,20},{18,... | collective-permute-start | bytes 1769480 | tf_op jit(solution)/shard_map/ppermute | solution.py:58
  121.3 14.5 %collective-permute-start.30 = (bf16[2,4,96,384]{3,2,1,0:T(8,128)(2,1)S(1)}, bf16[2,4,96,384]{3,2,1,0:T(8,128)(2,1)S(1)}, u32[]{:S(2)}, u32[]{:S(2)}) collective-permute-start(bf16[2,4,96,384]{3,2,1,0:T(8,128)(2,1)S(1)} %get-tuple-element.213), channel_id=1, source_target_pairs={{0,2},{2,0},{4,6},{6,4},{8,10},{10,8},{12,14},{14,12},{16,18},{18,... | collective-permute-start | bytes 1769480 | tf_op jit(solution)/shard_map/ppermute | solution.py:58
  154.1 36.9 %collective-permute-start.38 = (bf16[1,96,768]{2,1,0:T(8,128)(2,1)S(1)}, bf16[1,96,768]{2,1,0:T(8,128)(2,1)S(1)}, u32[]{:S(2)}, u32[]{:S(2)}) collective-permute-start(bf16[1,96,768]{2,1,0:T(8,128)(2,1)S(1)} %get-tuple-element.306), channel_id=1, source_target_pairs={{0,24},{2,26},{4,28},{6,30},{8,16},{10,18},{12,20},{14,22},{16,8},... | collective-permute-start | bytes 442376 | tf_op jit(solution)/shard_map/ppermute | solution.py:58
  156.7 34.4 %collective-permute-start.36 = (bf16[1,96,768]{2,1,0:T(8,128)(2,1)S(1)}, bf16[1,96,768]{2,1,0:T(8,128)(2,1)S(1)}, u32[]{:S(2)}, u32[]{:S(2)}) collective-permute-start(bf16[1,96,768]{2,1,0:T(8,128)(2,1)S(1)} %get-tuple-element.307), channel_id=1, source_target_pairs={{0,8},{2,10},{4,12},{6,14},{8,0},{10,2},{12,4},{14,6},{16,24},{18,... | collective-permute-start | bytes 442376 | tf_op jit(solution)/shard_map/ppermute | solution.py:58
  156.7 34.4 %collective-permute-start.37 = (bf16[1,96,768]{2,1,0:T(8,128)(2,1)S(1)}, bf16[1,96,768]{2,1,0:T(8,128)(2,1)S(1)}, u32[]{:S(2)}, u32[]{:S(2)}) collective-permute-start(bf16[1,96,768]{2,1,0:T(8,128)(2,1)S(1)} %get-tuple-element.308), channel_id=1, source_target_pairs={{0,16},{2,18},{4,20},{6,22},{8,24},{10,26},{12,28},{14,30},{16,0},... | collective-permute-start | bytes 442376 | tf_op jit(solution)/shard_map/ppermute | solution.py:58
  160.6 30.5 %collective-permute-start.39 = (bf16[2,4,48,896]{3,2,1,0:T(8,128)(2,1)S(1)}, bf16[2,4,48,896]{3,2,1,0:T(8,128)(2,1)S(1)}, u32[]{:S(2)}, u32[]{:S(2)}) collective-permute-start(bf16[2,4,48,896]{3,2,1,0:T(8,128)(2,1)S(1)} %pad_maximum_fusion.2), channel_id=1, source_target_pairs={{0,4},{2,6},{4,0},{6,2},{8,12},{10,14},{12,8},{14,10},{16,20},{18,... | collective-permute-start | bytes 2064392 | tf_op jit(solution)/shard_map/ppermute | solution.py:58
  162.2 28.9 %collective-permute-start.40 = (bf16[2,4,48,1024]{3,2,1,0:T(8,128)(2,1)S(1)}, bf16[2,4,48,1024]{3,2,1,0:T(8,128)(2,1)S(1)}, u32[]{:S(2)}, u32[]{:S(2)}) collective-permute-start(bf16[2,4,48,1024]{3,2,1,0:T(8,128)(2,1)S(1)} %pad_maximum_fusion), channel_id=1, source_target_pairs={{0,2},{2,0},{4,6},{6,4},{8,10},{10,8},{12,14},{14,12},{16,18},{18,... | collective-permute-start | bytes 2359304 | tf_op jit(solution)/shard_map/ppermute | solution.py:58
  191.0 23.5 %collective-permute-start.44 = (bf16[3,256,768]{2,1,0:T(8,128)(2,1)}, bf16[3,256,768]{2,1,0:T(8,128)(2,1)}, u32[]{:S(2)}, u32[]{:S(2)}) collective-permute-start(bf16[3,256,768]{2,1,0:T(8,128)(2,1)} %get-tuple-element.269), channel_id=1, source_target_pairs={{0,1},{1,0},{2,3},{3,2},{4,5},{5,4},{6,7},{7,6},{8,9},{9,8},{10,11... | collective-permute-start | bytes 3538952 | tf_op jit(solution)/shard_map/ppermute | solution.py:148
  213.6 18.4 %collective-permute-start.43 = (bf16[3,256,768]{2,1,0:T(8,128)(2,1)S(1)}, bf16[3,256,768]{2,1,0:T(8,128)(2,1)S(1)}, u32[]{:S(2)}, u32[]{:S(2)}) collective-permute-start(bf16[3,256,768]{2,1,0:T(8,128)(2,1)S(1)} %get-tuple-element.265), channel_id=1, source_target_pairs={{0,1},{1,0},{2,3},{3,2},{4,5},{5,4},{6,7},{7,6},{8,9},{9,8},{10,11... | collective-permute-start | bytes 3538952 | tf_op jit(solution)/shard_map/ppermute | solution.py:148
  218.0 14.0 %collective-permute-start.46 = (bf16[2,4,48,640]{3,2,1,0:T(8,128)(2,1)S(1)}, bf16[2,4,48,640]{3,2,1,0:T(8,128)(2,1)S(1)}, u32[]{:S(2)}, u32[]{:S(2)}) collective-permute-start(bf16[2,4,48,640]{3,2,1,0:T(8,128)(2,1)S(1)} %get-tuple-element.271), channel_id=1, source_target_pairs={{0,2},{2,0},{4,6},{6,4},{8,10},{10,8},{12,14},{14,12},{16,18},{18,... | collective-permute-start | bytes 1474568 | tf_op jit(solution)/shard_map/ppermute | solution.py:58
  219.3 17.2 %collective-permute-start.51 = (bf16[1,48,1920]{2,1,0:T(8,128)(2,1)S(1)}, bf16[1,48,1920]{2,1,0:T(8,128)(2,1)S(1)}, u32[]{:S(2)}, u32[]{:S(2)}) collective-permute-start(bf16[1,48,1920]{2,1,0:T(8,128)(2,1)S(1)} %get-tuple-element.303), channel_id=1, source_target_pairs={{0,24},{2,26},{4,28},{6,30},{8,16},{10,18},{12,20},{14,22},{16,8},... | collective-permute-start | bytes 552968 | tf_op jit(solution)/shard_map/ppermute | solution.py:58
  221.9 14.6 %collective-permute-start.49 = (bf16[1,48,1920]{2,1,0:T(8,128)(2,1)S(1)}, bf16[1,48,1920]{2,1,0:T(8,128)(2,1)S(1)}, u32[]{:S(2)}, u32[]{:S(2)}) collective-permute-start(bf16[1,48,1920]{2,1,0:T(8,128)(2,1)S(1)} %get-tuple-element.304), channel_id=1, source_target_pairs={{0,8},{2,10},{4,12},{6,14},{8,0},{10,2},{12,4},{14,6},{16,24},{18,... | collective-permute-start | bytes 552968 | tf_op jit(solution)/shard_map/ppermute | solution.py:58
  (111 other events, 813.4 us)
